TPU v7x, 128 devices: a whole 4x4x4 slice. The times are simulated.
128 devices in a mesh: ka: 16 (over z, y), wa: 8 (over x, core).
Axes of the slice: x: 4, y: 4, z: 4, core: 2. Of those that a mesh axis runs over, the one named last changes fastest.
Arguments:
- sigma_hist: bfloat16 [6, 2, 256, 153600], P(None, None, 'wa', 'ka'), may hold values from -6 to 6
- resid_hist: bfloat16 [6, 2, 256, 153600], P(None, None, 'wa', 'ka'), may hold values from -100 to 100
- sigma_new: bfloat16 [2, 256, 153600], P(None, 'wa', 'ka'), may hold values from -6 to 6
- resid_new: bfloat16 [2, 256, 153600], P(None, 'wa', 'ka'), may hold values from -100 to 100
- slot_order: int32 [6], replicated, may hold values from 0 to 5, each once
- freq_index: int32 [256], replicated, may hold values from -1024 to 1023, as said below
- freq_weight: float32 [256], replicated, may hold values from 0.02 to 0.2
Outputs:
- sigma_tau: float32 [256, 2, 153600], P(('ka', 'wa'))
- mixed_sigma: bfloat16 [2, 256, 153600], P(None, 'wa', 'ka')
- diis_coeffs: float32 [6], replicated
Inputs may be any that keep to these rules, and one draw needn't show every extreme that they name: A permutation; slot_order[0] names the oldest slot. `freq_index`: distinct values; both -1024 and 1023 occur.
All inputs are finite; a program needn't handle non-finite values.
Results may differ from a plain program's by a relative error of at most 0.017.
Values may be sent and summed in bfloat16 or wider, within the bound.
A program may use at most 128 MiB of HBM per device.

v0:
```python
import math

import jax
import jax.numpy as jnp
from jax import lax
from jax.sharding import PartitionSpec as P

NTAU = 256


def diis_weights(gram_matrix):
    factor = jnp.linalg.cholesky(gram_matrix)
    unit_vector = jnp.ones((gram_matrix.shape[0], 1), gram_matrix.dtype)
    halfway = lax.linalg.triangular_solve(factor, unit_vector, left_side=True, lower=True)
    solved = lax.linalg.triangular_solve(
        factor, halfway, left_side=True, lower=True, transpose_a=True
    )[:, 0]
    return solved / jnp.sum(solved)


def stacked_kernel(freq_index, freq_weight, tau_points, tau_count):
    odd_freq = 2 * freq_index + 1
    odd_tau = 2 * tau_points + 1
    phases = jnp.mod(odd_tau[:, None] * odd_freq[None, :], 4 * tau_count)
    angles = phases.astype(jnp.float32) * (math.pi / (2 * tau_count))
    kernel_re = (freq_weight[None, :] * jnp.cos(angles)).astype(jnp.bfloat16)
    kernel_im = (-freq_weight[None, :] * jnp.sin(angles)).astype(jnp.bfloat16)
    real_rows = jnp.concatenate([kernel_re, -kernel_im], axis=1)
    imag_rows = jnp.concatenate([kernel_im, kernel_re], axis=1)
    both = jnp.stack([real_rows, imag_rows], axis=1)
    return both.reshape(2 * tau_points.shape[0], 2 * freq_index.shape[0])


def apply_kernel(kernel, spectrum):
    flattened = spectrum.reshape(2 * spectrum.shape[1], spectrum.shape[2])
    result = jnp.dot(kernel, flattened, preferred_element_type=jnp.float32)
    return result.reshape(kernel.shape[0] // 2, 2, spectrum.shape[2])


def shards(sigma_hist, resid_hist, sigma_new, resid_new, slot_order, freq_index, freq_weight):
    history = sigma_hist.shape[0]
    chosen = (jnp.arange(history, dtype=jnp.int32) == slot_order[0]).astype(jnp.float32)
    keep_mask = 1.0 - chosen
    flat_hist = resid_hist.reshape(history, -1)
    flat_new = resid_new.reshape(1, -1)
    contract = (((1,), (1,)), ((), ()))
    hist_gram = lax.dot_general(flat_hist, flat_hist, contract, preferred_element_type=jnp.float32)
    against = lax.dot_general(flat_hist, flat_new, contract, preferred_element_type=jnp.float32)[
        :, 0
    ]
    itself = lax.dot_general(flat_new, flat_new, contract, preferred_element_type=jnp.float32)[0, 0]
    partial_gram = (
        keep_mask[:, None] * keep_mask[None, :] * hist_gram
        + keep_mask[:, None] * chosen[None, :] * against[:, None]
        + chosen[:, None] * keep_mask[None, :] * against[None, :]
        + chosen[:, None] * chosen[None, :] * itself
    )
    gram_matrix = lax.psum(partial_gram, ("ka", "wa"))
    diis_coeffs = diis_weights(gram_matrix)
    hist_weights = diis_coeffs * keep_mask
    new_weight = jnp.sum(diis_coeffs * chosen)
    summed = new_weight * (sigma_new.astype(jnp.float32) + resid_new.astype(jnp.float32))
    for member in range(history):
        summed = summed + hist_weights[member] * (
            sigma_hist[member].astype(jnp.float32) + resid_hist[member].astype(jnp.float32)
        )
    mixed_sigma = summed.astype(jnp.bfloat16)
    ka_count = lax.axis_size("ka")
    wa_count = lax.axis_size("wa")
    freq_local = sigma_new.shape[1]
    tau_share = NTAU // wa_count
    tau_block = tau_share // ka_count
    wa_position = lax.axis_index("wa")
    start_freq = wa_position * freq_local
    local_index = lax.dynamic_slice_in_dim(freq_index, start_freq, freq_local)
    local_weight = lax.dynamic_slice_in_dim(freq_weight, start_freq, freq_local)
    position = jnp.arange(lax.axis_size("wa") * tau_share, dtype=jnp.int32)
    owner_wa = position // tau_share
    within = position % tau_share
    tau_ids = (within // tau_block * wa_count + owner_wa) * tau_block + within % tau_block
    kernel = stacked_kernel(local_index, local_weight, tau_ids, NTAU)
    own_taus = lax.psum_scatter(
        apply_kernel(kernel, mixed_sigma).astype(jnp.bfloat16),
        "wa",
        scatter_dimension=0,
        tiled=True,
    ).astype(jnp.float32)
    sigma_tau = lax.all_to_all(
        own_taus.astype(jnp.bfloat16), "ka", split_axis=0, concat_axis=2, tiled=True
    ).astype(own_taus.dtype)
    return (sigma_tau, mixed_sigma, diis_coeffs)


def solution(mesh):
    return jax.shard_map(
        shards,
        mesh=mesh,
        in_specs=(
            P(None, None, "wa", "ka"),
            P(None, None, "wa", "ka"),
            P(None, "wa", "ka"),
            P(None, "wa", "ka"),
            P(),
            P(),
            P(),
        ),
        out_specs=(P(("ka", "wa"), None, None), P(None, "wa", "ka"), P()),
        check_vma=False,
    )
```

profile of v0, /device:TPU:1, one launch (start us, length us, event | category | flops | bytes accessed | tf_op | source)
XLA Modules:
  0.0 227.1 jit_solution(17851912660182626388)
XLA Ops:
  7.2 0.0 reduce-scatter.2.cloned.1.call-start
  7.2 0.7 broadcast_subtract_fusion
  7.9 0.7 compare_convert_fusion
  8.6 2.5 %fusion.4 = f32[]{:T(128)} fusion(bf16[2,32,9600]{2,1,0:T(8,128)(2,1)} %param.10), kind=kLoop, calls=%fused_computation.7 | loop fusion | flops 1843199 | bytes 1228804 | tf_op jit(solution)/shard_map/dot_general | solution.py:51
  11.1 12.4 %fusion.29 = f32[6]{0:T(128)S(1)} fusion(bf16[2,32,9600,1]{2,1,0,3:T(8,128)(2,1)} %bitcast.70, bf16[6,2,32,9600]{3,2,1,0:T(8,128)(2,1)} %param.8), kind=kOutput, calls=%fused_computation.23 | convolution fusion | flops 7372800 | bytes 8601624 | tf_op jit(solution)/shard_map/dot_general | solution.py:48
  23.4 0.0 copy-done.4
  23.4 0.1 fusion.55
  23.5 21.6 %fusion.26 = f32[6,6]{0,1:T(8,128)S(1)} fusion(bf16[6,2,32,9600]{3,2,1,0:T(8,128)(2,1)} %param.8, f32[]{:T(128)} %fusion.4, f32[6]{0:T(128)S(1)} %fusion.29, f32[6]{0:T(128)S(1)} %compare_convert_fusion, f32[6]{0:T(128)S(1)} %broadcast_subtract_fusion), kind=kOutput, calls=%fused_computation.22 | convolution fusion | flops 44237196 | bytes 7373020 | tf_op jit(solution)/shard_map/dot_general | solution.py:47
  45.1 0.0 copy-done.5
  45.1 0.1 multiply_add_fusion.1
  45.2 68.6 %psum.7 = f32[6,6]{0,1:T(8,128)S(1)} all-reduce(f32[6,6]{0,1:T(8,128)S(1)} %fusion.26), channel_id=1, replica_groups=mesh['ka'=16,'wa'=8] {'ka','wa'}, use_global_device_ids=true, to_apply=%region_0.0 | all-reduce | flops 36 | bytes 288 | tf_op jit(solution)/shard_map/psum | solution.py:58
  113.9 0.1 copy.19
  114.0 0.5 cholesky.16
  114.5 0.6 compare_reduce_fusion
  115.2 0.6 fusion.40
  115.8 0.5 custom-call.8
  116.3 0.1 convolution_bitcast_fusion.1
  116.4 0.8 fusion.57
  117.2 0.0 copy-done.2
  117.2 1.3 fusion.49
  118.5 0.7 fusion.56
  119.2 0.2 fusion.54
  119.4 0.2 multiply_convert_fusion
  119.6 11.4 %fusion.12 = bf16[2,32,9600]{2,1,0:T(8,128)(2,1)S(1)} fusion(bf16[2,32,9600]{2,1,0:T(8,128)(2,1)S(1)} %copy-done, bf16[2,32,9600]{2,1,0:T(8,128)(2,1)} %param.9, bf16[6,2,32,9600]{3,2,1,0:T(8,128)(2,1)} %param.8, bf16[6,2,32,9600]{3,2,1,0:T(8,128)(2,1)} %param.7, f32[]{:T(128)} %bitcast.24, f32[]{:T(128)} %bitcast.22, f32[]{:T(128)} %bitcast.20, ...), kind=kLoop, calls=%fused_computation.15 | loop fusion | flops 21504000 | bytes 18432028 | tf_op jit(solution)/shard_map/convert_element_type | solution.py:67
  131.0 0.0 copy-start.1
  131.0 5.3 %convolution_convert_fusion = bf16[256,2,9600]{2,0,1:T(8,128)(2,1)} fusion(bf16[64,9600,1]{1,0,2:T(8,128)(2,1)S(1)} %bitcast.72, bf16[256,1,64]{0,2,1:T(8,128)(2,1)S(1)} %get-tuple-element.8, bf16[256,1,64]{0,2,1:T(8,128)(2,1)S(1)} %get-tuple-element.7), kind=kOutput, calls=%fused_computation | convolution fusion | flops 634093568 | bytes 11124736 | tf_op jit(solution)/shard_map/dot_general | solution.py:36
  136.3 0.0 reduce-scatter.2.cloned.1.call-update
  136.3 55.3 %reduce-scatter.2.cloned.1.call-done = bf16[32,2,9600]{2,0,1:T(8,128)(2,1)} async-done(((bf16[256,2,9600]{2,0,1:T(8,128)(2,1)}), bf16[32,2,9600]{2,0,1:T(8,128)(2,1)}) %reduce-scatter.2.cloned.1.call-update) | async-done | bytes 1228816 | tf_op jit(solution)/shard_map/reduce_scatter | solution.py:82
  191.6 2.2 copy.21
  193.8 24.0 %all_to_all.4 = bf16[32,2,9600]{2,1,0:T(2,128)(2,1)S(1)} all-to-all(bf16[32,2,9600]{2,1,0:T(2,128)(2,1)S(1)} %copy.21), channel_id=1, replica_groups=mesh['ka'=16,'wa'=8] {'ka'}, dimensions={0} | all-to-all | bytes 2457600 | tf_op jit(solution)/shard_map/all_to_all | solution.py:88
  217.8 0.8 convert_bitcast_fusion
  218.6 1.6 copy.30
  (13 shorter events, 0.1 us)
Async XLA Ops:
  7.2 184.4 %reduce-scatter.2.cloned.1.call-start = ((), (), s32[]{:S(2)}) async-start(), calls=%async_computation.2 | async-start | bytes 11059200 | tf_op jit(solution)/shard_map/reduce_scatter | solution.py:82
  11.1 12.4 %copy-start.4 = (f32[256]{0:T(256)S(1)}, f32[256]{0:T(256)}, u32[]{:S(2)}) copy-start(f32[256]{0:T(256)} %param.13) | copy-start | bytes 3076
  23.5 21.6 %copy-start.5 = (s32[256]{0:T(256)S(1)}, s32[256]{0:T(256)}, u32[]{:S(2)}) copy-start(s32[256]{0:T(256)} %param.12) | copy-start | bytes 3076
  23.5 93.7 %copy-start.2 = (s32[6]{0:T(128)S(1)}, s32[6]{0:T(128)}, u32[]{:S(2)}) copy-start(s32[6]{0:T(128)} %param.11) | copy-start | bytes 76
  23.5 96.1 %copy-start = (bf16[2,32,9600]{2,1,0:T(8,128)(2,1)S(1)}, bf16[2,32,9600]{2,1,0:T(8,128)(2,1)}, u32[]{:S(2)}) copy-start(bf16[2,32,9600]{2,1,0:T(8,128)(2,1)} %param.10) | copy-start | bytes 3686404
  118.5 12.5 %copy-start.3 = (f32[6]{0:T(128)}, f32[6]{0:T(128)S(1)}, u32[]{:S(2)}) copy-start(f32[6]{0:T(128)S(1)} %get-tuple-element.6) | copy-start | bytes 76
  131.0 5.3 %copy-start.1 = (bf16[2,32,9600]{2,1,0:T(8,128)(2,1)}, bf16[2,32,9600]{2,1,0:T(8,128)(2,1)S(1)}, u32[]{:S(2)}) copy-start(bf16[2,32,9600]{2,1,0:T(8,128)(2,1)S(1)} %fusion.12) | copy-start | bytes 3686404
Sparse Core Ops, SparseCore 0:
  136.4 55.0 reduce-scatter.1
where the time goes:
time: 229 us; the launch traced here: 227 us
  blocking collectives  92.6 us (40%)
  waiting for transfers between devices  55.3 us (24%)
  matrix products  40.1 us (18%)
  other arithmetic  20.3 us (9%)
  between operations  14.1 us (6%)
  local copies, waits for them, and re-layouts  4.63 us (2%)
    psum x1, blocking collectives, shards(): gram_matrix = lax.psum(partial_gram, ('ka', 'wa'))  68.6 us
    reduce_scatter x1, waiting for transfers between devices, shards(): lax.psum_scatter(apply_kernel(kernel, mixed_sigma).astype(jnp.bfloat16),...  55.3 us
    all_to_all x1, blocking collectives, shards(): lax.all_to_all(own_taus.astype(jnp.bfloat16), 'ka', split_axis=0, concat_...  24 us
    dot_general x1, matrix products, shards(): lax.dot_general(flat_hist, flat_hist, contract, preferred_element_type=jn...  21.6 us
    dot_general x1, matrix products, shards(): lax.dot_general(flat_hist, flat_new, contract, preferred_element_type=jnp...  12.4 us
    convert_element_type x1, other arithmetic, shards(): mixed_sigma = summed.astype(jnp.bfloat16)  11.4 us
    dot_general x1, matrix products, apply_kernel(): result = jnp.dot(kernel, flattened, preferred_element_type=jnp.float32)  5.26 us
  transfers between devices with their start and end apart: 1, of which 1 were waited for; matrix products, arithmetic and copies ran while one was open for 0% of the time, Pallas kernels for 0%

commit v1 on v0

v1 whole, which is shorter than its diff:
```python
import functools
import math

import jax
import jax.numpy as jnp
from jax import lax
from jax.experimental import pallas as pl
from jax.experimental.pallas import tpu as pltpu
from jax.sharding import PartitionSpec as P

MESH = pl.DeviceIdType.MESH
BF16, F32 = jnp.bfloat16, jnp.float32

HIST = 6
NTAU = 256
ROWS = 32
KA, WA = 16, 8
TILES = 75
UNIT = 512
WIDTH = TILES * 128
GRAM_PARTS = 5
EXTRA = 3
EXTRA_START = (64, 68, 71)
EXTRA_SLOTS = 6
GROUPS = 4
GROUP = KA // GROUPS


def sine(x):
    x2 = x * x
    p = -1.0 / 39916800.0
    for factor in (1.0 / 362880.0, -1.0 / 5040.0, 1.0 / 120.0, -1.0 / 6.0, 1.0):
        p = p * x2 + factor
    return x * p


def cosine_of_phase(phase):
    z = 256 - jnp.abs(phase - 512)
    return -sine(z.astype(F32) * (math.pi / 512))


def build_transform(freq_ref, weight_ref, table):
    odd_freq = 2 * freq_ref[...].reshape(1, NTAU) + 1
    weight = weight_ref[...].reshape(1, NTAU)

    def block(b, _):
        row = b * 64 + lax.broadcasted_iota(jnp.int32, (64, NTAU), 0)
        odd_tau = 2 * (row >> 1) + 1
        part = row & 1
        base = odd_freq * odd_tau + 256 * part
        for other in range(2):
            phase = (base - 256 * other) & 1023
            table[pl.ds(pl.multiple_of(b * 64, 64), 64), other * NTAU : (other + 1) * NTAU] = (
                weight * cosine_of_phase(phase)
            ).astype(BF16)
        return 0

    lax.fori_loop(0, 2 * NTAU // 64, block, 0)


def build_regroup(regroup):
    out = lax.broadcasted_iota(jnp.int32, (128, 128), 0)
    source = ((out >> 1) & 3) * 32 + (out >> 4) * 4 + ((out >> 3) & 1) * 2 + (out & 1)
    here = lax.broadcasted_iota(jnp.int32, (128, 128), 1)
    regroup[...] = jnp.where(source == here, 1.0, 0.0).astype(BF16)


def solve(gram, oldest):
    def entry(s, u):
        return jnp.broadcast_to(gram[s : s + 1, u : u + 1], (8, 128))

    full = {(s, u): entry(s, u) for s in range(HIST + 1) for u in range(s + 1)}
    mat = {}
    for s in range(HIST):
        for u in range(s + 1):
            value = jnp.where(oldest == s, full[HIST, u], full[s, u])
            if s == u:
                value = jnp.where(oldest == s, full[HIST, HIST], full[s, s])
            else:
                value = jnp.where(oldest == u, full[HIST, s], value)
            mat[s, u] = value
    low, inv = {}, {}
    for s in range(HIST):
        for u in range(s + 1):
            value = mat[s, u]
            for w in range(u):
                value = value - low[s, w] * low[u, w]
            if s == u:
                inv[s] = 1.0 / jnp.sqrt(value)
            else:
                low[s, u] = value * inv[u]
    half = {}
    for s in range(HIST):
        value = jnp.ones((8, 128), F32)
        for u in range(s):
            value = value - low[s, u] * half[u]
        half[s] = value * inv[s]
    full_solution = {}
    for s in reversed(range(HIST)):
        value = half[s]
        for u in range(s + 1, HIST):
            value = value - low[u, s] * full_solution[u]
        full_solution[s] = value * inv[s]
    total = full_solution[0]
    for s in range(1, HIST):
        total = total + full_solution[s]
    return [full_solution[s] / total for s in range(HIST)]


def main_kernel(
    slot_ref, freq_ref, weight_ref, sig_hist, res_hist, sig_new, res_new,
    own, own_extra, mixed_out, coef_out,
    sig_v, res_v, sign_v, resn_v, weights, gx, gy, table, regroup,
    mixed, spectra, turned, spread, spread_extra,
    in_sem, gs_sem, gr_sem, s1, r1, s2, r2, s3, r3, out_sem, local_sem,
):
    k, i = lax.axis_index("ka"), lax.axis_index("wa")
    x, core = i // 2, i % 2
    z, y = k // 4, k % 4

    part = WIDTH // GRAM_PARTS
    reads = []
    for n in range(GRAM_PARTS):
        cols = pl.ds(n * part, part)
        reads.append(
            (
                pltpu.make_async_copy(res_hist.at[:, :, :, cols], res_v.at[:, :, :, cols], in_sem.at[0, n]),
                pltpu.make_async_copy(res_new.at[:, :, cols], resn_v.at[:, :, cols], in_sem.at[1, n]),
            )
        )
    sigma_reads = []
    for n, (start, size) in enumerate(((8192, 1408), (0, 4096), (4096, 4096))):
        cols = pl.ds(start, size)
        sigma_reads.append(
            (
                pltpu.make_async_copy(sig_hist.at[:, :, :, cols], sig_v.at[:, :, :, cols], in_sem.at[2, n]),
                pltpu.make_async_copy(sig_new.at[:, :, cols], sign_v.at[:, :, cols], in_sem.at[3, n]),
            )
        )
    for pair in reads + sigma_reads:
        for read in pair:
            read.start()

    barrier = pltpu.get_barrier_semaphore()

    def greet_wa(d, _):
        pl.semaphore_signal(barrier, inc=1, device_id=(k, (i + d) % WA), device_id_type=MESH)
        return 0

    def greet_ka(d, _):
        pl.semaphore_signal(barrier, inc=1, device_id=((k + d) % KA, i), device_id_type=MESH)
        return 0

    lax.fori_loop(1, WA, greet_wa, 0)
    lax.fori_loop(1, KA, greet_ka, 0)

    acc = jnp.zeros((7 * ROWS, 7 * ROWS), F32)
    for n in range(GRAM_PARTS):
        for read in reads[n]:
            read.wait()
        for ri in range(2):
            block = jnp.concatenate(
                [
                    res_v[:, ri, :, n * part : (n + 1) * part].reshape(HIST * ROWS, part),
                    resn_v[ri, :, n * part : (n + 1) * part],
                ],
                axis=0,
            )
            acc = acc + lax.dot_general(block, block, (((1,), (1,)), ((), ())), preferred_element_type=F32)
    rows = lax.broadcasted_iota(jnp.int32, acc.shape, 0)
    lanes = lax.broadcasted_iota(jnp.int32, acc.shape, 1)
    kept = jnp.where((rows & (ROWS - 1)) == (lanes & (ROWS - 1)), acc, 0.0)
    by_lane = jnp.sum(kept.reshape(7, ROWS, 7 * ROWS), axis=1)
    fold = jnp.where(
        lax.broadcasted_iota(jnp.int32, (7 * ROWS, 128), 0) // ROWS
        == lax.broadcasted_iota(jnp.int32, (7 * ROWS, 128), 1),
        1.0,
        0.0,
    )
    share = jnp.dot(by_lane, fold, preferred_element_type=F32, precision=lax.Precision.HIGHEST)
    gx[i] = jnp.concatenate([share, jnp.zeros((1, 128), F32)], axis=0)

    pl.semaphore_wait(barrier, WA - 1 + KA - 1)

    def share_wa(d):
        return pltpu.make_async_remote_copy(
            src_ref=gx.at[i], dst_ref=gx.at[i], send_sem=gs_sem.at[0, d], recv_sem=gr_sem.at[0, d],
            device_id=(k, (i + d) % WA), device_id_type=MESH)

    def share_ka(d):
        return pltpu.make_async_remote_copy(
            src_ref=gy.at[k], dst_ref=gy.at[k], send_sem=gs_sem.at[1, d], recv_sem=gr_sem.at[1, d],
            device_id=((k + d) % KA, i), device_id_type=MESH)

    def each(low, high, do):
        def step(d, _):
            do(d)
            return 0

        lax.fori_loop(low, high, step, 0)

    each(1, WA, lambda d: share_wa(d).start())
    build_transform(freq_ref, weight_ref, table)
    build_regroup(regroup)
    each(1, WA, lambda d: share_wa(d).wait())
    total = gx[0]
    for n in range(1, WA):
        total = total + gx[n]
    gy[k] = total
    each(1, KA, lambda d: share_ka(d).start())
    each(1, KA, lambda d: share_ka(d).wait())
    gram = gy[0]
    for n in range(1, KA):
        gram = gram + gy[n]

    oldest = slot_ref[0]
    coeffs = solve(gram, oldest)
    lane = lax.broadcasted_iota(jnp.int32, (8, 128), 1)
    packed = jnp.zeros((8, 128), F32)
    newest = jnp.zeros((8, 128), F32)
    for s in range(HIST):
        packed = jnp.where(lane == s, coeffs[s], packed)
        newest = jnp.where(oldest == s, coeffs[s], newest)
        weights[s] = jnp.where(oldest == s, 0.0, coeffs[s])
    weights[HIST] = newest
    coef_out[...] = packed

    def mix(unit, start):
        def rows_of(h, _):
            ri, low = h // 2, pl.multiple_of((h % 2) * 16, 16)
            for tile in range(4):
                cols = pl.ds(pl.multiple_of(start + tile * 128, 128), 128)
                at = (ri, pl.ds(low, 16), cols)
                w = weights[HIST]
                both = jnp.concatenate([w, w], axis=0)
                total = both * (sign_v[at].astype(F32) + resn_v[at].astype(F32))
                for s in range(HIST):
                    w = weights[s]
                    both = jnp.concatenate([w, w], axis=0)
                    total = total + both * (sig_v[(s, *at)].astype(F32) + res_v[(s, *at)].astype(F32))
                mixed[unit, ri, pl.ds(low, 16), tile * 128 : (tile + 1) * 128] = total.astype(BF16)
            return 0

        lax.fori_loop(0, 4, rows_of, 0)

    def unit_copy(c, d):
        j = (i + d) % WA
        return pltpu.make_async_remote_copy(
            src_ref=mixed.at[c * WA + j], dst_ref=spectra.at[c, :, i],
            send_sem=s1.at[c, d], recv_sem=r1.at[c, d], device_id=(k, j), device_id_type=MESH)

    def unit_keep(c):
        return pltpu.make_async_copy(mixed.at[c * WA + i], spectra.at[c, :, i], local_sem.at[0, c])

    def owner_of(m):
        return 2 * ((m + y) % 4) + z % 2

    def extra_copy(m):
        return pltpu.make_async_remote_copy(
            src_ref=mixed.at[2 * WA + m], dst_ref=spectra.at[2, :, i],
            send_sem=s1.at[2, m], recv_sem=r1.at[2, i], device_id=(k, owner_of(m)), device_id_type=MESH)

    def extra_keep(m):
        return pltpu.make_async_copy(mixed.at[2 * WA + m], spectra.at[2, :, i], local_sem.at[0, 2])

    def extra_arrival(n):
        return pltpu.make_async_remote_copy(
            src_ref=mixed.at[2 * WA], dst_ref=spectra.at[2, :, n],
            send_sem=s1.at[2, 0], recv_sem=r1.at[2, n], device_id=(k, n), device_id_type=MESH)

    writes = []
    for n, (unit, skip) in enumerate([(u, 0) for u in range(18)] + [(18, 128)]):
        start = unit * UNIT if unit < 16 else EXTRA_START[unit - 16] * 128
        writes.append(
            pltpu.make_async_copy(
                mixed.at[unit, :, :, skip:UNIT],
                mixed_out.at[:, :, start + skip : start + UNIT],
                out_sem.at[n],
            )
        )

    for read in sigma_reads[0]:
        read.wait()
    for m in range(EXTRA):
        mix(2 * WA + m, EXTRA_START[m] * 128)

        @pl.when(owner_of(m) == i)
        def _(m=m):
            extra_keep(m).start()

        @pl.when(owner_of(m) != i)
        def _(m=m):
            extra_copy(m).start()

    for c in range(2):
        for read in sigma_reads[1 + c]:
            read.wait()

        def send_unit(d, c=c):
            unit = c * WA + (i + d) % WA
            mix(unit, unit * UNIT)

            @pl.when(d == 0)
            def _():
                unit_keep(c).start()

            @pl.when(d != 0)
            def _():
                unit_copy(c, d).start()

        each(0, WA, send_unit)
    for write in writes:
        write.start()

    def transform(c):
        values = jnp.dot(table[...], spectra[c].reshape(2 * NTAU, UNIT), preferred_element_type=F32).astype(BF16)
        for b in range(4):
            stacked = jnp.concatenate(
                [
                    jnp.concatenate(
                        [values[(4 * b + n) * 32 : (4 * b + n + 1) * 32, a * 128 : (a + 1) * 128] for a in range(4)],
                        axis=0,
                    )
                    for n in range(4)
                ],
                axis=1,
            )
            grouped = jnp.dot(regroup[...], stacked, preferred_element_type=F32).astype(BF16)
            for n in range(4):
                turned[c, 4 * b + n] = grouped[:, n * 128 : (n + 1) * 128].reshape(WA, 16, 128)

    def times_copy(c, d):
        peer = (k + d) % KA
        return pltpu.make_async_remote_copy(
            src_ref=turned.at[c, peer], dst_ref=spread.at[c, d],
            send_sem=s2.at[c, d], recv_sem=r2.at[c, d], device_id=(peer, i), device_id_type=MESH)

    def times_keep(c):
        return pltpu.make_async_copy(turned.at[c, k], spread.at[c, 0], local_sem.at[1, c])

    extra_m = (x - y + 4) % 4
    is_owner = jnp.logical_and(z % 2 == core, extra_m < EXTRA)
    my_slot = (z // 2) * EXTRA + extra_m

    def slot_source(s):
        return 4 * (2 * (s // EXTRA) + core) + (x - s % EXTRA + 4) % 4

    def extra_times_copy(d):
        peer = (k + d) % KA
        return pltpu.make_async_remote_copy(
            src_ref=turned.at[2, peer], dst_ref=spread_extra.at[my_slot],
            send_sem=s2.at[2, d], recv_sem=r2.at[2, my_slot], device_id=(peer, i), device_id_type=MESH)

    def extra_times_keep():
        return pltpu.make_async_copy(turned.at[2, k], spread_extra.at[my_slot], local_sem.at[1, 2])

    def extra_times_arrival(s):
        return pltpu.make_async_remote_copy(
            src_ref=turned.at[2, 0], dst_ref=spread_extra.at[s],
            send_sem=s2.at[2, 0], recv_sem=r2.at[2, s], device_id=(slot_source(s), i), device_id_type=MESH)

    def owner_copy(c, g, e):
        j = (i + e) % WA
        ds = pl.ds(g * GROUP, GROUP)
        return pltpu.make_async_remote_copy(
            src_ref=spread.at[c, ds, j], dst_ref=own.at[c, i, ds],
            send_sem=s3.at[c, g, e], recv_sem=r3.at[c, g, e], device_id=(k, j), device_id_type=MESH)

    def owner_keep(c, g):
        ds = pl.ds(g * GROUP, GROUP)
        return pltpu.make_async_copy(spread.at[c, ds, i], own.at[c, i, ds], s3.at[c, g, 0])

    def extra_owner_copy(e):
        j = (i + e) % WA
        return pltpu.make_async_remote_copy(
            src_ref=spread_extra.at[:, j], dst_ref=own_extra.at[i],
            send_sem=s3.at[2, 0, e], recv_sem=r3.at[2, 0, e], device_id=(k, j), device_id_type=MESH)

    def extra_owner_keep():
        return pltpu.make_async_copy(spread_extra.at[:, i], own_extra.at[i], s3.at[2, 0, 0])

    @pl.when(is_owner)
    def _():
        extra_keep(0).wait()
        for d in range(1, WA):
            extra_arrival((i + d) % WA).wait_recv()
        transform(2)
        extra_times_keep().start()
        each(1, KA, lambda d: extra_times_copy(d).start())

    def first_stage(c):
        unit_keep(c).wait()
        each(1, WA, lambda d: unit_copy(c, d).wait_recv())
        transform(c)
        times_keep(c).start()
        each(1, KA, lambda d: times_copy(c, d).start())

    def last_stage(c):
        times_keep(c).wait()

        def group(g):
            def arrived(d):
                @pl.when(d != 0)
                def _():
                    times_copy(c, d).wait_recv()

            each(g * GROUP, (g + 1) * GROUP, arrived)
            each(1, WA, lambda e: owner_copy(c, g, e).start())
            owner_keep(c, g).start()

        each(0, GROUPS, group)

    first_stage(0)

    @pl.when(is_owner)
    def _():
        extra_times_keep().wait()

    def extra_arrived(s):
        @pl.when(slot_source(s) != k)
        def _():
            extra_times_arrival(s).wait_recv()

    each(0, EXTRA_SLOTS, extra_arrived)
    each(1, WA, lambda e: extra_owner_copy(e).start())
    extra_owner_keep().start()

    first_stage(1)
    last_stage(0)
    last_stage(1)

    for m in range(EXTRA):

        @pl.when(owner_of(m) != i)
        def _(m=m):
            extra_copy(m).wait_send()

    for c in range(2):
        each(1, WA, lambda d, c=c: unit_copy(c, d).wait_send())
        each(1, KA, lambda d, c=c: times_copy(c, d).wait_send())

    @pl.when(is_owner)
    def _():
        each(1, KA, lambda d: extra_times_copy(d).wait_send())

    for write in writes:
        write.wait()
    extra_owner_keep().wait()
    each(1, WA, lambda e: extra_owner_copy(e).wait())
    for c in range(2):

        def finish(g, c=c):
            owner_keep(c, g).wait()
            each(1, WA, lambda e: owner_copy(c, g, e).wait())

        each(0, GROUPS, finish)


def last_kernel(own, own_extra, mixed_in, coef_in, out, mixed_out, coef_out, times, out_sem):
    k, i = lax.axis_index("ka"), lax.axis_index("wa")
    passed = pltpu.make_async_copy(mixed_in, mixed_out, out_sem.at[2])
    passed.start()
    coef_out[...] = coef_in[0, :HIST]

    def place(value, tile):
        value = value.astype(F32)
        at = pl.ds(2 * tile, 8)
        times[0, at] = value[:8]
        times[1, at] = value[8:]

    def from_row(d, _):
        row = (k - d + KA) % KA
        for c in range(2):
            for n in range(WA):
                place(own[c, n, d], row * TILES + (c * WA + n) * 4)
        return 0

    lax.fori_loop(0, KA, from_row, 0)

    for n in range(WA):
        x, core = n // 2, n % 2
        for s in range(EXTRA_SLOTS):
            m = s % EXTRA
            row = 4 * (2 * (s // EXTRA) + core) + (x - m) % 4
            place(own_extra[n, s], row * TILES + EXTRA_START[m])
    writes = [pltpu.make_async_copy(times.at[t], out.at[t], out_sem.at[t]) for t in range(2)]
    for write in writes:
        write.start()
    for write in writes:
        write.wait()
    passed.wait()


def shards(sigma_hist, resid_hist, sigma_new, resid_new, slot_order, freq_index, freq_weight):
    vmem = pl.BlockSpec(memory_space=pltpu.VMEM)
    hbm = pl.BlockSpec(memory_space=pl.ANY)
    smem = pl.BlockSpec(memory_space=pltpu.SMEM)
    dma = pltpu.SemaphoreType.DMA
    own, own_extra, mixed, coeffs = pl.pallas_call(
        main_kernel,
        out_shape=(
            jax.ShapeDtypeStruct((2, WA, KA, 16, 128), BF16),
            jax.ShapeDtypeStruct((WA, EXTRA_SLOTS, 16, 128), BF16),
            jax.ShapeDtypeStruct(sigma_new.shape, BF16),
            jax.ShapeDtypeStruct((8, 128), F32),
        ),
        in_specs=[smem, vmem, vmem, hbm, hbm, hbm, hbm],
        out_specs=(hbm, hbm, hbm, vmem),
        scratch_shapes=[
            pltpu.VMEM(sigma_hist.shape, BF16),
            pltpu.VMEM(resid_hist.shape, BF16),
            pltpu.VMEM(sigma_new.shape, BF16),
            pltpu.VMEM(resid_new.shape, BF16),
            pltpu.VMEM((HIST + 1, 8, 128), F32),
            pltpu.VMEM((WA, 8, 128), F32),
            pltpu.VMEM((KA, 8, 128), F32),
            pltpu.VMEM((2 * NTAU, 2 * NTAU), BF16),
            pltpu.VMEM((128, 128), BF16),
            pltpu.VMEM((2 * WA + EXTRA, 2, ROWS, UNIT), BF16),
            pltpu.VMEM((3, 2, WA, ROWS, UNIT), BF16),
            pltpu.VMEM((3, KA, WA, 16, 128), BF16),
            pltpu.VMEM((2, KA, WA, 16, 128), BF16),
            pltpu.VMEM((EXTRA_SLOTS, WA, 16, 128), BF16),
            dma((4, GRAM_PARTS)),
            dma((2, KA)),
            dma((2, KA)),
            dma((3, WA)),
            dma((3, WA)),
            dma((3, KA)),
            dma((3, KA)),
            dma((3, GROUPS, WA)),
            dma((3, GROUPS, WA)),
            dma((2 * WA + EXTRA,)),
            dma((2, 3)),
        ],
        compiler_params=pltpu.CompilerParams(
            collective_id=0, has_side_effects=True, vmem_limit_bytes=48 * 2**20
        ),
        name="mix_and_transform",
    )(slot_order, freq_index, freq_weight, sigma_hist, resid_hist, sigma_new, resid_new)
    out, mixed_sigma, diis_coeffs = pl.pallas_call(
        last_kernel,
        out_shape=(
            jax.ShapeDtypeStruct((2, KA * TILES * 2, 128), F32),
            jax.ShapeDtypeStruct(sigma_new.shape, BF16),
            jax.ShapeDtypeStruct((HIST,), F32),
        ),
        in_specs=[vmem, vmem, hbm, vmem],
        out_specs=(hbm, hbm, vmem),
        scratch_shapes=[pltpu.VMEM((2, KA * TILES * 2, 128), F32), dma((3,))],
        compiler_params=pltpu.CompilerParams(vmem_limit_bytes=16 * 2**20),
        name="unpack",
    )(own, own_extra, mixed, coeffs)
    sigma_tau = out.reshape(2, KA * TILES, 2, 128).transpose(0, 2, 1, 3).reshape(2, 2, KA * WIDTH)
    return (sigma_tau, mixed_sigma, diis_coeffs)


def solution(mesh):
    return jax.shard_map(
        shards,
        mesh=mesh,
        in_specs=(
            P(None, None, "wa", "ka"),
            P(None, None, "wa", "ka"),
            P(None, "wa", "ka"),
            P(None, "wa", "ka"),
            P(),
            P(),
            P(),
        ),
        out_specs=(P(("ka", "wa"), None, None), P(None, "wa", "ka"), P()),
        check_vma=False,
    )
```

time: 229 us -> 65.1 us (0.28)
  blocking collectives: 92.6 us -> 0 us
  Pallas kernels: 0 us -> 59.6 us
  waiting for transfers between devices: 55.3 us -> 0 us
  matrix products: 40.1 us -> 0 us
  other arithmetic: 20.3 us -> 0 us
  between operations: 14.1 us -> 0.65 us
    psum x1 -> x0, blocking collectives: 68.6 us -> none  [shards(): gram_matrix = lax.psum(partial_gram, ('ka', 'wa'))]
    pallas_call x0 -> x2, Pallas kernels: none -> 59.6 us  [the longest x1 57.3 us: shards(): pl.pallas_call(main_kernel, out_shape=(jax.ShapeDtypeStruct((2, WA, KA, 1...]
    reduce_scatter x1 -> x0, waiting for transfers between devices: 55.3 us -> none  [shards(): lax.psum_scatter(apply_kernel(kernel, mixed_sigma).astype(jnp.bfloat16),...]
    dot_general x3 -> x0, matrix products: 39.2 us -> none  [the longest x1 21.6 us: shards(): lax.dot_general(flat_hist, flat_hist, contract, preferred_element_type=jn...]
    all_to_all x1 -> x0, blocking collectives: 24 us -> none  [shards(): lax.all_to_all(own_taus.astype(jnp.bfloat16), 'ka', split_axis=0, concat_...]
    convert_element_type x3 -> x0, other arithmetic: 12.2 us -> none  [the longest x1 11.4 us: shards(): mixed_sigma = summed.astype(jnp.bfloat16)]
    unnamed x12 -> x10, local copies, waits for them, and re-layouts: 0.02 us -> 4.58 us
    dot_general x1 -> x0, other arithmetic: 2.53 us -> none  [shards(): lax.dot_general(flat_new, flat_new, contract, preferred_element_type=jnp....]
  transfers between devices with their start and end apart: 1 -> 0, of which waited for: 1 -> 0; matrix products, arithmetic and copies ran while one was open for 0% -> 0% of each run, Pallas kernels for 0% -> 0%
where the time goes in v1:
time: 65.1 us; the launch traced here: 64.9 us
  Pallas kernels  59.6 us (92%)
  local copies, waits for them, and re-layouts  4.58 us (7%)
    pallas_call x1, Pallas kernels, shards(): pl.pallas_call(main_kernel, out_shape=(jax.ShapeDtypeStruct((2, WA, KA, 1...  57.3 us
    unnamed x10, local copies, waits for them, and re-layouts  4.58 us
    pallas_call x1, Pallas kernels, shards(): pl.pallas_call(last_kernel, out_shape=(jax.ShapeDtypeStruct((2, KA * TILE...  2.38 us

profile of v1, /device:TPU:1, one launch (start us, length us, event | category | flops | bytes accessed | tf_op | source)
XLA Modules:
  0.0 64.9 jit_solution(14650802465758019335)
XLA Ops:
  0.6 0.0 copy-start
  0.6 1.3 %copy-done = bf16[2,32,9600]{2,1,0:T(8,128)(2,1)S(1)} copy-done((bf16[2,32,9600]{2,1,0:T(8,128)(2,1)S(1)}, bf16[2,32,9600]{2,1,0:T(8,128)(2,1)}, u32[]{:S(2)}) %copy-start) | copy-done | bytes 1228824
  1.9 0.0 copy-start.1
  1.9 1.3 %copy-done.1 = bf16[2,32,9600]{2,1,0:T(8,128)(2,1)S(1)} copy-done((bf16[2,32,9600]{2,1,0:T(8,128)(2,1)S(1)}, bf16[2,32,9600]{2,1,0:T(8,128)(2,1)}, u32[]{:S(2)}) %copy-start.1) | copy-done | bytes 1228824
  3.2 0.0 copy-start.2
  3.2 0.7 %copy-done.2 = s32[256]{0:T(256)S(1)} copy-done((s32[256]{0:T(256)S(1)}, s32[256]{0:T(256)}, u32[]{:S(2)}) %copy-start.2) | copy-done | bytes 1048
  3.9 0.0 copy-start.3
  3.9 0.7 %copy-done.3 = f32[256]{0:T(256)S(1)} copy-done((f32[256]{0:T(256)S(1)}, f32[256]{0:T(256)}, u32[]{:S(2)}) %copy-start.3) | copy-done | bytes 1048
  4.6 0.0 copy-start.4
  4.6 0.7 %copy-done.4 = s32[6]{0:T(128)S(1)} copy-done((s32[6]{0:T(128)S(1)}, s32[6]{0:T(128)}, u32[]{:S(2)}) %copy-start.4) | copy-done | bytes 48
  5.2 57.3 %mix_and_transform.1 = (bf16[2,8,16,16,128]{4,3,2,1,0:T(8,128)(2,1)S(1)}, bf16[8,6,16,128]{3,2,1,0:T(8,128)(2,1)S(1)}, bf16[2,32,9600]{2,1,0:T(8,128)(2,1)S(1)}, f32[8,128]{1,0:T(8,128)S(1)}) custom-call(s32[6]{0:T(128)S(1)} %copy-done.4, s32[256]{0:T(256)S(1)} %copy-done.2, f32[256]{0:T(256)S(1)} %copy-done.3, bf16[6,2,32,9600]{3,2,1,0:T(8,128)(2,1)} %sig_hist.1, ...), custom_call_target="tpu_custom_call" | custom-call | tf_op jit(solution)/shard_map/mix_and_transform/pallas_call | solution.py:499
  62.5 2.4 %unpack.1 = (f32[2,2400,128]{2,1,0:T(8,128)}, bf16[2,32,9600]{2,1,0:T(8,128)(2,1)}, f32[6]{0:T(128)}) custom-call(bf16[2,8,16,16,128]{4,3,2,1,0:T(8,128)(2,1)S(1)} %get-tuple-element.10.own, bf16[8,6,16,128]{3,2,1,0:T(8,128)(2,1)S(1)} %get-tuple-element.11.own_extra, bf16[2,32,9600]{2,1,0:T(8,128)(2,1)S(1)} %get-tuple-element.12.mixed_in, ...), custom_call_target="tpu_custom_call" | custom-call | tf_op jit(solution)/shard_map/unpack/pallas_call | solution.py:541
Async XLA Ops:
  0.6 1.3 %copy-start = (bf16[2,32,9600]{2,1,0:T(8,128)(2,1)S(1)}, bf16[2,32,9600]{2,1,0:T(8,128)(2,1)}, u32[]{:S(2)}) copy-start(bf16[2,32,9600]{2,1,0:T(8,128)(2,1)} %sig_new.1) | copy-start | bytes 3686404
  1.9 1.3 %copy-start.1 = (bf16[2,32,9600]{2,1,0:T(8,128)(2,1)S(1)}, bf16[2,32,9600]{2,1,0:T(8,128)(2,1)}, u32[]{:S(2)}) copy-start(bf16[2,32,9600]{2,1,0:T(8,128)(2,1)} %res_new.1) | copy-start | bytes 3686404
  3.2 0.7 %copy-start.2 = (s32[256]{0:T(256)S(1)}, s32[256]{0:T(256)}, u32[]{:S(2)}) copy-start(s32[256]{0:T(256)} %freq_ref.1) | copy-start | bytes 3076
  3.9 0.7 %copy-start.3 = (f32[256]{0:T(256)S(1)}, f32[256]{0:T(256)}, u32[]{:S(2)}) copy-start(f32[256]{0:T(256)} %weight_ref.1) | copy-start | bytes 3076
  4.6 0.7 %copy-start.4 = (s32[6]{0:T(128)S(1)}, s32[6]{0:T(128)}, u32[]{:S(2)}) copy-start(s32[6]{0:T(128)} %slot_ref.1) | copy-start | bytes 76

commit v2 on v1

--- a/solution.py
+++ b/solution.py
@@ -18,12 +18,15 @@
 TILES = 75
 UNIT = 512
 WIDTH = TILES * 128
-GRAM_PARTS = 5
+GRAM_PARTS = ((0, 50), (50, 25))
+GRAM_STEP = 25
 EXTRA = 3
 EXTRA_START = (64, 68, 71)
 EXTRA_SLOTS = 6
 GROUPS = 4
 GROUP = KA // GROUPS
+OFFSETS = ((2, 2), (2, 1), (2, 3), (2, 0), (1, 2), (3, 2), (1, 1), (3, 3), (1, 3), (3, 1), (1, 0), (3, 0), (0, 2), (0, 1), (0, 3))
+GROUP_ORDER = (2, 1, 3, 0)
 
 
 def sine(x):
@@ -39,9 +42,9 @@
     return -sine(z.astype(F32) * (math.pi / 512))
 
 
-def build_transform(freq_ref, weight_ref, table):
-    odd_freq = 2 * freq_ref[...].reshape(1, NTAU) + 1
-    weight = weight_ref[...].reshape(1, NTAU)
+def build_transform(small, table):
+    odd_freq = 2 * jnp.concatenate([small[0:1], small[1:2]], axis=1).astype(jnp.int32) + 1
+    weight = jnp.concatenate([small[2:3], small[3:4]], axis=1)
 
     def block(b, _):
         row = b * 64 + lax.broadcasted_iota(jnp.int32, (64, NTAU), 0)
@@ -108,20 +111,29 @@
 
 
 def main_kernel(
-    slot_ref, freq_ref, weight_ref, sig_hist, res_hist, sig_new, res_new,
+    small, sig_hist, res_hist, sig_new, res_new,
     own, own_extra, mixed_out, coef_out,
-    sig_v, res_v, sign_v, resn_v, weights, gx, gy, table, regroup,
+    sig_v, res_v, sign_v, resn_v, acc, weights, gx, gy, table, regroup,
     mixed, spectra, turned, spread, spread_extra,
-    in_sem, gs_sem, gr_sem, s1, r1, s2, r2, s3, r3, out_sem, local_sem,
+    in_sem, share_sem, s1, r1, se, s2, r2, r2e, s3, r3, out_sem, local_sem,
 ):
     k, i = lax.axis_index("ka"), lax.axis_index("wa")
     x, core = i // 2, i % 2
     z, y = k // 4, k % 4
 
-    part = WIDTH // GRAM_PARTS
+    def each(low, high, do):
+        def step(d, _):
+            do(d)
+            return 0
+
+        lax.fori_loop(low, high, step, 0)
+
+    def arrived(ref, sem):
+        pltpu.make_async_copy(ref, ref, sem).wait()
+
     reads = []
-    for n in range(GRAM_PARTS):
-        cols = pl.ds(n * part, part)
+    for n, (start, size) in enumerate(GRAM_PARTS):
+        cols = pl.ds(start * 128, size * 128)
         reads.append(
             (
                 pltpu.make_async_copy(res_hist.at[:, :, :, cols], res_v.at[:, :, :, cols], in_sem.at[0, n]),
@@ -137,8 +149,8 @@
                 pltpu.make_async_copy(sig_new.at[:, :, cols], sign_v.at[:, :, cols], in_sem.at[3, n]),
             )
         )
-    for pair in reads + sigma_reads:
-        for read in pair:
+    for group in reads:
+        for read in group:
             read.start()
 
     barrier = pltpu.get_barrier_semaphore()
@@ -154,22 +166,29 @@
     lax.fori_loop(1, WA, greet_wa, 0)
     lax.fori_loop(1, KA, greet_ka, 0)
 
-    acc = jnp.zeros((7 * ROWS, 7 * ROWS), F32)
-    for n in range(GRAM_PARTS):
+    acc[...] = jnp.zeros_like(acc)
+    for n, (start, size) in enumerate(GRAM_PARTS):
         for read in reads[n]:
             read.wait()
-        for ri in range(2):
-            block = jnp.concatenate(
-                [
-                    res_v[:, ri, :, n * part : (n + 1) * part].reshape(HIST * ROWS, part),
-                    resn_v[ri, :, n * part : (n + 1) * part],
-                ],
-                axis=0,
-            )
-            acc = acc + lax.dot_general(block, block, (((1,), (1,)), ((), ())), preferred_element_type=F32)
+
+        def add_products(b, start=start):
+            cols = pl.ds(pl.multiple_of((start + b * GRAM_STEP) * 128, 128), GRAM_STEP * 128)
+            total = None
+            for ri in range(2):
+                block = jnp.concatenate(
+                    [res_v[:, ri, :, cols].reshape(HIST * ROWS, GRAM_STEP * 128), resn_v[ri, :, cols]], axis=0
+                )
+                product = lax.dot_general(block, block, (((1,), (1,)), ((), ())), preferred_element_type=F32)
+                total = product if total is None else total + product
+            acc[...] += total
+
+        each(0, size // GRAM_STEP, add_products)
+    for pair in sigma_reads:
+        for read in pair:
+            read.start()
     rows = lax.broadcasted_iota(jnp.int32, acc.shape, 0)
     lanes = lax.broadcasted_iota(jnp.int32, acc.shape, 1)
-    kept = jnp.where((rows & (ROWS - 1)) == (lanes & (ROWS - 1)), acc, 0.0)
+    kept = jnp.where((rows & (ROWS - 1)) == (lanes & (ROWS - 1)), acc[...], 0.0)
     by_lane = jnp.sum(kept.reshape(7, ROWS, 7 * ROWS), axis=1)
     fold = jnp.where(
         lax.broadcasted_iota(jnp.int32, (7 * ROWS, 128), 0) // ROWS
@@ -184,36 +203,31 @@
 
     def share_wa(d):
         return pltpu.make_async_remote_copy(
-            src_ref=gx.at[i], dst_ref=gx.at[i], send_sem=gs_sem.at[0, d], recv_sem=gr_sem.at[0, d],
+            src_ref=gx.at[i], dst_ref=gx.at[i], send_sem=share_sem.at[0], recv_sem=share_sem.at[1],
             device_id=(k, (i + d) % WA), device_id_type=MESH)
 
     def share_ka(d):
         return pltpu.make_async_remote_copy(
-            src_ref=gy.at[k], dst_ref=gy.at[k], send_sem=gs_sem.at[1, d], recv_sem=gr_sem.at[1, d],
+            src_ref=gy.at[k], dst_ref=gy.at[k], send_sem=share_sem.at[2], recv_sem=share_sem.at[3],
             device_id=((k + d) % KA, i), device_id_type=MESH)
 
-    def each(low, high, do):
-        def step(d, _):
-            do(d)
-            return 0
-
-        lax.fori_loop(low, high, step, 0)
-
     each(1, WA, lambda d: share_wa(d).start())
-    build_transform(freq_ref, weight_ref, table)
+    build_transform(small, table)
     build_regroup(regroup)
-    each(1, WA, lambda d: share_wa(d).wait())
+    for n in range(2):
+        arrived(gx.at[: WA - 1], share_sem.at[n])
     total = gx[0]
     for n in range(1, WA):
         total = total + gx[n]
     gy[k] = total
     each(1, KA, lambda d: share_ka(d).start())
-    each(1, KA, lambda d: share_ka(d).wait())
+    for n in range(2, 4):
+        arrived(gy.at[: KA - 1], share_sem.at[n])
     gram = gy[0]
     for n in range(1, KA):
         gram = gram + gy[n]
 
-    oldest = slot_ref[0]
+    oldest = jnp.broadcast_to(small[4:5, 0:1], (8, 128))
     coeffs = solve(gram, oldest)
     lane = lax.broadcasted_iota(jnp.int32, (8, 128), 1)
     packed = jnp.zeros((8, 128), F32)
@@ -247,7 +261,7 @@
         j = (i + d) % WA
         return pltpu.make_async_remote_copy(
             src_ref=mixed.at[c * WA + j], dst_ref=spectra.at[c, :, i],
-            send_sem=s1.at[c, d], recv_sem=r1.at[c, d], device_id=(k, j), device_id_type=MESH)
+            send_sem=s1.at[c], recv_sem=r1.at[c], device_id=(k, j), device_id_type=MESH)
 
     def unit_keep(c):
         return pltpu.make_async_copy(mixed.at[c * WA + i], spectra.at[c, :, i], local_sem.at[0, c])
@@ -258,24 +272,19 @@
     def extra_copy(m):
         return pltpu.make_async_remote_copy(
             src_ref=mixed.at[2 * WA + m], dst_ref=spectra.at[2, :, i],
-            send_sem=s1.at[2, m], recv_sem=r1.at[2, i], device_id=(k, owner_of(m)), device_id_type=MESH)
+            send_sem=se.at[m], recv_sem=r1.at[2], device_id=(k, owner_of(m)), device_id_type=MESH)
 
     def extra_keep(m):
         return pltpu.make_async_copy(mixed.at[2 * WA + m], spectra.at[2, :, i], local_sem.at[0, 2])
 
-    def extra_arrival(n):
-        return pltpu.make_async_remote_copy(
-            src_ref=mixed.at[2 * WA], dst_ref=spectra.at[2, :, n],
-            send_sem=s1.at[2, 0], recv_sem=r1.at[2, n], device_id=(k, n), device_id_type=MESH)
-
     writes = []
-    for n, (unit, skip) in enumerate([(u, 0) for u in range(18)] + [(18, 128)]):
+    for unit, skip in [(u, 0) for u in range(18)] + [(18, 128)]:
         start = unit * UNIT if unit < 16 else EXTRA_START[unit - 16] * 128
         writes.append(
             pltpu.make_async_copy(
                 mixed.at[unit, :, :, skip:UNIT],
                 mixed_out.at[:, :, start + skip : start + UNIT],
-                out_sem.at[n],
+                out_sem,
             )
         )
 
@@ -313,13 +322,16 @@
         write.start()
 
     def transform(c):
-        values = jnp.dot(table[...], spectra[c].reshape(2 * NTAU, UNIT), preferred_element_type=F32).astype(BF16)
-        for b in range(4):
+        def block(b):
+            values = jnp.dot(
+                table[pl.ds(pl.multiple_of(b * 128, 128), 128)],
+                spectra[c].reshape(2 * NTAU, UNIT),
+                preferred_element_type=F32,
+            ).astype(BF16)
             stacked = jnp.concatenate(
                 [
                     jnp.concatenate(
-                        [values[(4 * b + n) * 32 : (4 * b + n + 1) * 32, a * 128 : (a + 1) * 128] for a in range(4)],
-                        axis=0,
+                        [values[n * 32 : (n + 1) * 32, a * 128 : (a + 1) * 128] for a in range(4)], axis=0
                     )
                     for n in range(4)
                 ],
@@ -329,11 +341,16 @@
             for n in range(4):
                 turned[c, 4 * b + n] = grouped[:, n * 128 : (n + 1) * 128].reshape(WA, 16, 128)
 
+        each(0, 4, block)
+
+    def peer_at(d):
+        return (z + d // 4) % 4 * 4 + (y + d % 4) % 4
+
     def times_copy(c, d):
-        peer = (k + d) % KA
+        peer = peer_at(d)
         return pltpu.make_async_remote_copy(
             src_ref=turned.at[c, peer], dst_ref=spread.at[c, d],
-            send_sem=s2.at[c, d], recv_sem=r2.at[c, d], device_id=(peer, i), device_id_type=MESH)
+            send_sem=s2.at[c], recv_sem=r2.at[c, d // GROUP], device_id=(peer, i), device_id_type=MESH)
 
     def times_keep(c):
         return pltpu.make_async_copy(turned.at[c, k], spread.at[c, 0], local_sem.at[1, c])
@@ -346,10 +363,10 @@
         return 4 * (2 * (s // EXTRA) + core) + (x - s % EXTRA + 4) % 4
 
     def extra_times_copy(d):
-        peer = (k + d) % KA
+        peer = peer_at(d)
         return pltpu.make_async_remote_copy(
             src_ref=turned.at[2, peer], dst_ref=spread_extra.at[my_slot],
-            send_sem=s2.at[2, d], recv_sem=r2.at[2, my_slot], device_id=(peer, i), device_id_type=MESH)
+            send_sem=s2.at[2], recv_sem=r2e.at[my_slot], device_id=(peer, i), device_id_type=MESH)
 
     def extra_times_keep():
         return pltpu.make_async_copy(turned.at[2, k], spread_extra.at[my_slot], local_sem.at[1, 2])
@@ -357,58 +374,52 @@
     def extra_times_arrival(s):
         return pltpu.make_async_remote_copy(
             src_ref=turned.at[2, 0], dst_ref=spread_extra.at[s],
-            send_sem=s2.at[2, 0], recv_sem=r2.at[2, s], device_id=(slot_source(s), i), device_id_type=MESH)
+            send_sem=s2.at[2], recv_sem=r2e.at[s], device_id=(slot_source(s), i), device_id_type=MESH)
 
     def owner_copy(c, g, e):
         j = (i + e) % WA
         ds = pl.ds(g * GROUP, GROUP)
         return pltpu.make_async_remote_copy(
             src_ref=spread.at[c, ds, j], dst_ref=own.at[c, i, ds],
-            send_sem=s3.at[c, g, e], recv_sem=r3.at[c, g, e], device_id=(k, j), device_id_type=MESH)
+            send_sem=s3.at[c], recv_sem=r3.at[c], device_id=(k, j), device_id_type=MESH)
 
     def owner_keep(c, g):
         ds = pl.ds(g * GROUP, GROUP)
-        return pltpu.make_async_copy(spread.at[c, ds, i], own.at[c, i, ds], s3.at[c, g, 0])
+        return pltpu.make_async_copy(spread.at[c, ds, i], own.at[c, i, ds], local_sem.at[2, c])
 
     def extra_owner_copy(e):
         j = (i + e) % WA
         return pltpu.make_async_remote_copy(
             src_ref=spread_extra.at[:, j], dst_ref=own_extra.at[i],
-            send_sem=s3.at[2, 0, e], recv_sem=r3.at[2, 0, e], device_id=(k, j), device_id_type=MESH)
+            send_sem=s3.at[2], recv_sem=r3.at[2], device_id=(k, j), device_id_type=MESH)
 
     def extra_owner_keep():
-        return pltpu.make_async_copy(spread_extra.at[:, i], own_extra.at[i], s3.at[2, 0, 0])
+        return pltpu.make_async_copy(spread_extra.at[:, i], own_extra.at[i], local_sem.at[2, 2])
 
     @pl.when(is_owner)
     def _():
         extra_keep(0).wait()
-        for d in range(1, WA):
-            extra_arrival((i + d) % WA).wait_recv()
+        arrived(spectra.at[2, :, : WA - 1], r1.at[2])
         transform(2)
         extra_times_keep().start()
-        each(1, KA, lambda d: extra_times_copy(d).start())
+        for dz, dy in OFFSETS:
+            extra_times_copy(dz * 4 + dy).start()
 
     def first_stage(c):
         unit_keep(c).wait()
-        each(1, WA, lambda d: unit_copy(c, d).wait_recv())
+        arrived(spectra.at[c, :, : WA - 1], r1.at[c])
         transform(c)
         times_keep(c).start()
-        each(1, KA, lambda d: times_copy(c, d).start())
+        for dz, dy in OFFSETS:
+            times_copy(c, dz * 4 + dy).start()
 
     def last_stage(c):
-        times_keep(c).wait()
-
-        def group(g):
-            def arrived(d):
-                @pl.when(d != 0)
-                def _():
-                    times_copy(c, d).wait_recv()
-
-            each(g * GROUP, (g + 1) * GROUP, arrived)
-            each(1, WA, lambda e: owner_copy(c, g, e).start())
+        for g in GROUP_ORDER:
+            if g == 0:
+                times_keep(c).wait()
+            arrived(spread.at[c, max(1, g * GROUP) : (g + 1) * GROUP], r2.at[c, g])
+            each(1, WA, lambda e, g=g: owner_copy(c, g, e).start())
             owner_keep(c, g).start()
-
-        each(0, GROUPS, group)
 
     first_stage(0)
 
@@ -436,56 +447,53 @@
             extra_copy(m).wait_send()
 
     for c in range(2):
-        each(1, WA, lambda d, c=c: unit_copy(c, d).wait_send())
-        each(1, KA, lambda d, c=c: times_copy(c, d).wait_send())
+        arrived(spectra.at[c, :, : WA - 1], s1.at[c])
+        arrived(turned.at[c, : KA - 1], s2.at[c])
 
     @pl.when(is_owner)
     def _():
-        each(1, KA, lambda d: extra_times_copy(d).wait_send())
-
-    for write in writes:
-        write.wait()
+        arrived(turned.at[2, : KA - 1], s2.at[2])
+
+    arrived(mixed_out, out_sem)
     extra_owner_keep().wait()
-    each(1, WA, lambda e: extra_owner_copy(e).wait())
+    for sem in (s3, r3):
+        arrived(own_extra.at[: WA - 1], sem.at[2])
     for c in range(2):
-
-        def finish(g, c=c):
-            owner_keep(c, g).wait()
-            each(1, WA, lambda e: owner_copy(c, g, e).wait())
-
-        each(0, GROUPS, finish)
-
-
-def last_kernel(own, own_extra, mixed_in, coef_in, out, mixed_out, coef_out, times, out_sem):
-    k, i = lax.axis_index("ka"), lax.axis_index("wa")
-    passed = pltpu.make_async_copy(mixed_in, mixed_out, out_sem.at[2])
+        arrived(own.at[c, 0], local_sem.at[2, c])
+        for sem in (s3, r3):
+            arrived(own.at[c, : WA - 1], sem.at[c])
+
+
+def last_kernel(own, own_extra, mixed, coef_in, out, mixed_out, coef_out, times, out_sem):
+    k = lax.axis_index("ka")
+    z, y = k // 4, k % 4
+    passed = pltpu.make_async_copy(mixed, mixed_out, out_sem.at[4])
     passed.start()
     coef_out[...] = coef_in[0, :HIST]
 
     def place(value, tile):
         value = value.astype(F32)
-        at = pl.ds(2 * tile, 8)
-        times[0, at] = value[:8]
-        times[1, at] = value[8:]
-
-    def from_row(d, _):
-        row = (k - d + KA) % KA
-        for c in range(2):
-            for n in range(WA):
-                place(own[c, n, d], row * TILES + (c * WA + n) * 4)
-        return 0
-
-    lax.fori_loop(0, KA, from_row, 0)
-
-    for n in range(WA):
-        x, core = n // 2, n % 2
-        for s in range(EXTRA_SLOTS):
-            m = s % EXTRA
-            row = 4 * (2 * (s // EXTRA) + core) + (x - m) % 4
-            place(own_extra[n, s], row * TILES + EXTRA_START[m])
-    writes = [pltpu.make_async_copy(times.at[t], out.at[t], out_sem.at[t]) for t in range(2)]
-    for write in writes:
-        write.start()
+        times[0, pl.ds(2 * tile, 8)] = value[:8]
+        times[1, pl.ds(2 * tile, 8)] = value[8:]
+
+    writes = []
+    for row_z in range(4):
+        core = row_z % 2
+
+        def row(row_y, _, row_z=row_z, core=core):
+            slot = (z - row_z + 4) % 4 * GROUP + (y - row_y + 4) % 4
+            first = (4 * row_z + row_y) * TILES
+            for c in range(2):
+                for n in range(WA):
+                    place(own[c, n, slot], first + (c * WA + n) * 4)
+            for m in range(EXTRA):
+                place(own_extra[2 * ((row_y + m) % 4) + core, row_z // 2 * EXTRA + m], first + EXTRA_START[m])
+            return 0
+
+        lax.fori_loop(0, 4, row, 0)
+        rows = pl.ds(row_z * GROUP * TILES * 2, GROUP * TILES * 2)
+        writes.append(pltpu.make_async_copy(times.at[:, rows], out.at[:, rows], out_sem.at[row_z]))
+        writes[-1].start()
     for write in writes:
         write.wait()
     passed.wait()
@@ -493,9 +501,13 @@
 
 def shards(sigma_hist, resid_hist, sigma_new, resid_new, slot_order, freq_index, freq_weight):
     vmem = pl.BlockSpec(memory_space=pltpu.VMEM)
-    hbm = pl.BlockSpec(memory_space=pl.ANY)
-    smem = pl.BlockSpec(memory_space=pltpu.SMEM)
+    hbm = pl.BlockSpec(memory_space=pltpu.HBM)
     dma = pltpu.SemaphoreType.DMA
+    small = (
+        jnp.pad(freq_index.astype(F32), (0, 384))
+        + jnp.pad(freq_weight, (256, 128))
+        + jnp.pad(slot_order.astype(F32), (512, 128 - HIST))
+    ).reshape(5, 128)
     own, own_extra, mixed, coeffs = pl.pallas_call(
         main_kernel,
         out_shape=(
@@ -504,13 +516,14 @@
             jax.ShapeDtypeStruct(sigma_new.shape, BF16),
             jax.ShapeDtypeStruct((8, 128), F32),
         ),
-        in_specs=[smem, vmem, vmem, hbm, hbm, hbm, hbm],
+        in_specs=[vmem] + [hbm] * 4,
         out_specs=(hbm, hbm, hbm, vmem),
         scratch_shapes=[
             pltpu.VMEM(sigma_hist.shape, BF16),
             pltpu.VMEM(resid_hist.shape, BF16),
             pltpu.VMEM(sigma_new.shape, BF16),
             pltpu.VMEM(resid_new.shape, BF16),
+            pltpu.VMEM((7 * ROWS, 7 * ROWS), F32),
             pltpu.VMEM((HIST + 1, 8, 128), F32),
             pltpu.VMEM((WA, 8, 128), F32),
             pltpu.VMEM((KA, 8, 128), F32),
@@ -521,23 +534,24 @@
             pltpu.VMEM((3, KA, WA, 16, 128), BF16),
             pltpu.VMEM((2, KA, WA, 16, 128), BF16),
             pltpu.VMEM((EXTRA_SLOTS, WA, 16, 128), BF16),
-            dma((4, GRAM_PARTS)),
-            dma((2, KA)),
-            dma((2, KA)),
-            dma((3, WA)),
-            dma((3, WA)),
-            dma((3, KA)),
-            dma((3, KA)),
-            dma((3, GROUPS, WA)),
-            dma((3, GROUPS, WA)),
-            dma((2 * WA + EXTRA,)),
-            dma((2, 3)),
+            dma((4, 3)),
+            dma((4,)),
+            dma((2,)),
+            dma((3,)),
+            dma((EXTRA,)),
+            dma((3,)),
+            dma((2, GROUPS)),
+            dma((EXTRA_SLOTS,)),
+            dma((3,)),
+            dma((3,)),
+            dma,
+            dma((3, 3)),
         ],
         compiler_params=pltpu.CompilerParams(
-            collective_id=0, has_side_effects=True, vmem_limit_bytes=48 * 2**20
+            collective_id=0, has_side_effects=True, vmem_limit_bytes=51 * 2**20
         ),
         name="mix_and_transform",
-    )(slot_order, freq_index, freq_weight, sigma_hist, resid_hist, sigma_new, resid_new)
+    )(small, sigma_hist, resid_hist, sigma_new, resid_new)
     out, mixed_sigma, diis_coeffs = pl.pallas_call(
         last_kernel,
         out_shape=(
@@ -545,9 +559,12 @@
             jax.ShapeDtypeStruct(sigma_new.shape, BF16),
             jax.ShapeDtypeStruct((HIST,), F32),
         ),
-        in_specs=[vmem, vmem, hbm, vmem],
+        in_specs=[vmem] * 4,
         out_specs=(hbm, hbm, vmem),
-        scratch_shapes=[pltpu.VMEM((2, KA * TILES * 2, 128), F32), dma((3,))],
+        scratch_shapes=[
+            pltpu.VMEM((2, KA * TILES * 2, 128), F32),
+            dma((5,)),
+        ],
         compiler_params=pltpu.CompilerParams(vmem_limit_bytes=16 * 2**20),
         name="unpack",
     )(own, own_extra, mixed, coeffs)

time: 65.1 us -> 61.4 us (0.943)
  local copies, waits for them, and re-layouts: 4.58 us -> 0 us
  other arithmetic: 0 us -> 2.02 us
  Pallas kernels: 59.6 us -> 58.6 us
    unnamed x10 -> x0, local copies, waits for them, and re-layouts: 4.58 us -> none
    convert_element_type x0 -> x2, other arithmetic: none -> 1.34 us  [the longest x1 0.68 us: shards(): freq_index.astype(F32)]
    pallas_call x1, Pallas kernels: 57.3 us -> 56.2 us  [shards(): pl.pallas_call(main_kernel, out_shape=(jax.ShapeDtypeStruct((2, WA, KA, 1...]
    reshape x0 -> x1, other arithmetic: none -> 0.69 us  [shards(): small = (jnp.pad(freq_index.astype(F32), (0, 384)) + jnp.pad(freq_weight,...]
where the time goes in v2:
time: 61.4 us; the launch traced here: 61.2 us
  Pallas kernels  58.6 us (95%)
  other arithmetic  2.02 us (3%)
  between operations  0.64 us (1%)
    pallas_call x1, Pallas kernels, shards(): pl.pallas_call(main_kernel, out_shape=(jax.ShapeDtypeStruct((2, WA, KA, 1...  56.2 us
    pallas_call x1, Pallas kernels, shards(): pl.pallas_call(last_kernel, out_shape=(jax.ShapeDtypeStruct((2, KA * TILE...  2.39 us

profile of v2, /device:TPU:1, one launch (start us, length us, event | category | flops | bytes accessed | tf_op | source)
XLA Modules:
  0.0 61.2 jit_solution(5349598123290075761)
XLA Ops:
  0.6 0.7 %convert_element_type.13 = f32[6]{0:T(128)S(1)} convert(s32[6]{0:T(128)} %param.11) | non-fusion elementwise | flops 6 | bytes 48 | tf_op jit(solution)/shard_map/convert_element_type | solution.py:509
  1.3 0.7 %convert_element_type.12 = f32[256]{0:T(256)S(1)} convert(s32[256]{0:T(256)} %param.12) | non-fusion elementwise | flops 256 | bytes 2048 | tf_op jit(solution)/shard_map/convert_element_type | solution.py:507
  2.0 0.7 %add_bitcast_fusion.small = f32[5,128]{1,0:T(8,128)S(1)} fusion(f32[6]{0:T(128)S(1)} %convert_element_type.13, f32[256]{0:T(256)} %param.13, f32[256]{0:T(256)S(1)} %convert_element_type.12), kind=kLoop, calls=%fused_computation | loop fusion | flops 1280 | bytes 4632 | tf_op jit(solution)/shard_map/reshape | solution.py:510
  2.7 56.2 %mix_and_transform.1 = (bf16[2,8,16,16,128]{4,3,2,1,0:T(8,128)(2,1)S(1)}, bf16[8,6,16,128]{3,2,1,0:T(8,128)(2,1)S(1)}, bf16[2,32,9600]{2,1,0:T(8,128)(2,1)S(1)}, f32[8,128]{1,0:T(8,128)S(1)}) custom-call(f32[5,128]{1,0:T(8,128)S(1)} %add_bitcast_fusion.small, bf16[6,2,32,9600]{3,2,1,0:T(8,128)(2,1)} %sig_hist.1, bf16[6,2,32,9600]{3,2,1,0:T(8,128)(2,1)} %res_hist.1, ...), custom_call_target="tpu_custom_call" | custom-call | tf_op jit(solution)/shard_map/mix_and_transform/pallas_call | solution.py:511
  58.8 2.4 %unpack.1 = (f32[2,2400,128]{2,1,0:T(8,128)}, bf16[2,32,9600]{2,1,0:T(8,128)(2,1)}, f32[6]{0:T(128)}) custom-call(bf16[2,8,16,16,128]{4,3,2,1,0:T(8,128)(2,1)S(1)} %get-tuple-element.10.own, bf16[8,6,16,128]{3,2,1,0:T(8,128)(2,1)S(1)} %get-tuple-element.11.own_extra, bf16[2,32,9600]{2,1,0:T(8,128)(2,1)S(1)} %get-tuple-element.12.mixed, ...), custom_call_target="tpu_custom_call" | custom-call | tf_op jit(solution)/shard_map/unpack/pallas_call | solution.py:555

commit v3 on v2

--- a/solution.py
+++ b/solution.py
@@ -22,11 +22,6 @@
 GRAM_STEP = 25
 EXTRA = 3
 EXTRA_START = (64, 68, 71)
-EXTRA_SLOTS = 6
-GROUPS = 4
-GROUP = KA // GROUPS
-OFFSETS = ((2, 2), (2, 1), (2, 3), (2, 0), (1, 2), (3, 2), (1, 1), (3, 3), (1, 3), (3, 1), (1, 0), (3, 0), (0, 2), (0, 1), (0, 3))
-GROUP_ORDER = (2, 1, 3, 0)
 
 
 def sine(x):
@@ -114,8 +109,8 @@
     small, sig_hist, res_hist, sig_new, res_new,
     own, own_extra, mixed_out, coef_out,
     sig_v, res_v, sign_v, resn_v, acc, weights, gx, gy, table, regroup,
-    mixed, spectra, turned, spread, spread_extra,
-    in_sem, share_sem, s1, r1, se, s2, r2, r2e, s3, r3, out_sem, local_sem,
+    mixed, spectra, turned,
+    in_sem, share_sem, s1, r1, se, s2, r2, out_sem, local_sem,
 ):
     k, i = lax.axis_index("ka"), lax.axis_index("wa")
     x, core = i // 2, i % 2
@@ -339,106 +334,42 @@
             )
             grouped = jnp.dot(regroup[...], stacked, preferred_element_type=F32).astype(BF16)
             for n in range(4):
-                turned[c, 4 * b + n] = grouped[:, n * 128 : (n + 1) * 128].reshape(WA, 16, 128)
+                turned[c, pl.ds((4 * b + n) * WA, WA)] = grouped[:, n * 128 : (n + 1) * 128].reshape(WA, 16, 128)
 
         each(0, 4, block)
 
-    def peer_at(d):
-        return (z + d // 4) % 4 * 4 + (y + d % 4) % 4
-
-    def times_copy(c, d):
-        peer = peer_at(d)
-        return pltpu.make_async_remote_copy(
-            src_ref=turned.at[c, peer], dst_ref=spread.at[c, d],
-            send_sem=s2.at[c], recv_sem=r2.at[c, d // GROUP], device_id=(peer, i), device_id_type=MESH)
-
-    def times_keep(c):
-        return pltpu.make_async_copy(turned.at[c, k], spread.at[c, 0], local_sem.at[1, c])
-
+    me = k * WA + i
     extra_m = (x - y + 4) % 4
     is_owner = jnp.logical_and(z % 2 == core, extra_m < EXTRA)
-    my_slot = (z // 2) * EXTRA + extra_m
-
-    def slot_source(s):
-        return 4 * (2 * (s // EXTRA) + core) + (x - s % EXTRA + 4) % 4
-
-    def extra_times_copy(d):
-        peer = peer_at(d)
+
+    def times_copy(c, n):
+        d = KA * WA - n
+        pk = (z + d // 32) % 4 * 4 + (y + d // 8 % 4) % 4
+        pi = (x + d // 2 % 4) % 4 * 2 + (core + d % 2) % 2
+        target = own_extra.at[k * EXTRA + extra_m] if c == 2 else own.at[c, me]
         return pltpu.make_async_remote_copy(
-            src_ref=turned.at[2, peer], dst_ref=spread_extra.at[my_slot],
-            send_sem=s2.at[2], recv_sem=r2e.at[my_slot], device_id=(peer, i), device_id_type=MESH)
-
-    def extra_times_keep():
-        return pltpu.make_async_copy(turned.at[2, k], spread_extra.at[my_slot], local_sem.at[1, 2])
-
-    def extra_times_arrival(s):
-        return pltpu.make_async_remote_copy(
-            src_ref=turned.at[2, 0], dst_ref=spread_extra.at[s],
-            send_sem=s2.at[2], recv_sem=r2e.at[s], device_id=(slot_source(s), i), device_id_type=MESH)
-
-    def owner_copy(c, g, e):
-        j = (i + e) % WA
-        ds = pl.ds(g * GROUP, GROUP)
-        return pltpu.make_async_remote_copy(
-            src_ref=spread.at[c, ds, j], dst_ref=own.at[c, i, ds],
-            send_sem=s3.at[c], recv_sem=r3.at[c], device_id=(k, j), device_id_type=MESH)
-
-    def owner_keep(c, g):
-        ds = pl.ds(g * GROUP, GROUP)
-        return pltpu.make_async_copy(spread.at[c, ds, i], own.at[c, i, ds], local_sem.at[2, c])
-
-    def extra_owner_copy(e):
-        j = (i + e) % WA
-        return pltpu.make_async_remote_copy(
-            src_ref=spread_extra.at[:, j], dst_ref=own_extra.at[i],
-            send_sem=s3.at[2], recv_sem=r3.at[2], device_id=(k, j), device_id_type=MESH)
-
-    def extra_owner_keep():
-        return pltpu.make_async_copy(spread_extra.at[:, i], own_extra.at[i], local_sem.at[2, 2])
+            src_ref=turned.at[c, pk * WA + pi], dst_ref=target,
+            send_sem=s2.at[c], recv_sem=r2.at[c], device_id=(pk, pi), device_id_type=MESH)
+
+    def times_keep(c):
+        target = own_extra.at[k * EXTRA + extra_m] if c == 2 else own.at[c, me]
+        return pltpu.make_async_copy(turned.at[c, me], target, local_sem.at[1, c])
+
+    def send_times(c):
+        transform(c)
+        each(1, KA * WA, lambda n: times_copy(c, n).start())
+        times_keep(c).start()
 
     @pl.when(is_owner)
     def _():
         extra_keep(0).wait()
         arrived(spectra.at[2, :, : WA - 1], r1.at[2])
-        transform(2)
-        extra_times_keep().start()
-        for dz, dy in OFFSETS:
-            extra_times_copy(dz * 4 + dy).start()
-
-    def first_stage(c):
+        send_times(2)
+
+    for c in range(2):
         unit_keep(c).wait()
         arrived(spectra.at[c, :, : WA - 1], r1.at[c])
-        transform(c)
-        times_keep(c).start()
-        for dz, dy in OFFSETS:
-            times_copy(c, dz * 4 + dy).start()
-
-    def last_stage(c):
-        for g in GROUP_ORDER:
-            if g == 0:
-                times_keep(c).wait()
-            arrived(spread.at[c, max(1, g * GROUP) : (g + 1) * GROUP], r2.at[c, g])
-            each(1, WA, lambda e, g=g: owner_copy(c, g, e).start())
-            owner_keep(c, g).start()
-
-    first_stage(0)
-
-    @pl.when(is_owner)
-    def _():
-        extra_times_keep().wait()
-
-    def extra_arrived(s):
-        @pl.when(slot_source(s) != k)
-        def _():
-            extra_times_arrival(s).wait_recv()
-
-    each(0, EXTRA_SLOTS, extra_arrived)
-    each(1, WA, lambda e: extra_owner_copy(e).start())
-    extra_owner_keep().start()
-
-    first_stage(1)
-    last_stage(0)
-    last_stage(1)
+        send_times(c)
 
     for m in range(EXTRA):
 
@@ -448,25 +379,26 @@
 
     for c in range(2):
         arrived(spectra.at[c, :, : WA - 1], s1.at[c])
-        arrived(turned.at[c, : KA - 1], s2.at[c])
+
+    arrived(mixed_out, out_sem)
 
     @pl.when(is_owner)
     def _():
-        arrived(turned.at[2, : KA - 1], s2.at[2])
-
-    arrived(mixed_out, out_sem)
-    extra_owner_keep().wait()
-    for sem in (s3, r3):
-        arrived(own_extra.at[: WA - 1], sem.at[2])
+        times_keep(2).wait()
+        arrived(turned.at[2, : KA * WA - 1], s2.at[2])
+        arrived(own_extra.at[: KA * EXTRA - 1], r2.at[2])
+
+    @pl.when(jnp.logical_not(is_owner))
+    def _():
+        arrived(own_extra, r2.at[2])
+
     for c in range(2):
-        arrived(own.at[c, 0], local_sem.at[2, c])
-        for sem in (s3, r3):
-            arrived(own.at[c, : WA - 1], sem.at[c])
+        times_keep(c).wait()
+        arrived(turned.at[c, : KA * WA - 1], s2.at[c])
+        arrived(own.at[c, : KA * WA - 1], r2.at[c])
 
 
 def last_kernel(own, own_extra, mixed, coef_in, out, mixed_out, coef_out, times, out_sem):
-    k = lax.axis_index("ka")
-    z, y = k // 4, k % 4
     passed = pltpu.make_async_copy(mixed, mixed_out, out_sem.at[4])
     passed.start()
     coef_out[...] = coef_in[0, :HIST]
@@ -477,22 +409,20 @@
         times[1, pl.ds(2 * tile, 8)] = value[8:]
 
     writes = []
-    for row_z in range(4):
-        core = row_z % 2
-
-        def row(row_y, _, row_z=row_z, core=core):
-            slot = (z - row_z + 4) % 4 * GROUP + (y - row_y + 4) % 4
-            first = (4 * row_z + row_y) * TILES
+    for part in range(4):
+
+        def row(n, _, part=part):
+            k = 4 * part + n
             for c in range(2):
-                for n in range(WA):
-                    place(own[c, n, slot], first + (c * WA + n) * 4)
+                for i in range(WA):
+                    place(own[c, k * WA + i], k * TILES + (c * WA + i) * 4)
             for m in range(EXTRA):
-                place(own_extra[2 * ((row_y + m) % 4) + core, row_z // 2 * EXTRA + m], first + EXTRA_START[m])
+                place(own_extra[k * EXTRA + m], k * TILES + EXTRA_START[m])
             return 0
 
         lax.fori_loop(0, 4, row, 0)
-        rows = pl.ds(row_z * GROUP * TILES * 2, GROUP * TILES * 2)
-        writes.append(pltpu.make_async_copy(times.at[:, rows], out.at[:, rows], out_sem.at[row_z]))
+        rows = pl.ds(part * 4 * TILES * 2, 4 * TILES * 2)
+        writes.append(pltpu.make_async_copy(times.at[:, rows], out.at[:, rows], out_sem.at[part]))
         writes[-1].start()
     for write in writes:
         write.wait()
@@ -511,8 +441,8 @@
     own, own_extra, mixed, coeffs = pl.pallas_call(
         main_kernel,
         out_shape=(
-            jax.ShapeDtypeStruct((2, WA, KA, 16, 128), BF16),
-            jax.ShapeDtypeStruct((WA, EXTRA_SLOTS, 16, 128), BF16),
+            jax.ShapeDtypeStruct((2, KA * WA, 16, 128), BF16),
+            jax.ShapeDtypeStruct((KA * EXTRA, 16, 128), BF16),
             jax.ShapeDtypeStruct(sigma_new.shape, BF16),
             jax.ShapeDtypeStruct((8, 128), F32),
         ),
@@ -531,21 +461,16 @@
             pltpu.VMEM((128, 128), BF16),
             pltpu.VMEM((2 * WA + EXTRA, 2, ROWS, UNIT), BF16),
             pltpu.VMEM((3, 2, WA, ROWS, UNIT), BF16),
-            pltpu.VMEM((3, KA, WA, 16, 128), BF16),
-            pltpu.VMEM((2, KA, WA, 16, 128), BF16),
-            pltpu.VMEM((EXTRA_SLOTS, WA, 16, 128), BF16),
+            pltpu.VMEM((3, KA * WA, 16, 128), BF16),
             dma((4, 3)),
             dma((4,)),
             dma((2,)),
             dma((3,)),
             dma((EXTRA,)),
             dma((3,)),
-            dma((2, GROUPS)),
-            dma((EXTRA_SLOTS,)),
-            dma((3,)),
             dma((3,)),
             dma,
-            dma((3, 3)),
+            dma((2, 3)),
         ],
         compiler_params=pltpu.CompilerParams(
             collective_id=0, has_side_effects=True, vmem_limit_bytes=51 * 2**20

time: 61.4 us -> 56.2 us (0.915)
  Pallas kernels: 58.6 us -> 53.4 us
    pallas_call x1, Pallas kernels: 56.2 us -> 51 us  [shards(): pl.pallas_call(main_kernel, out_shape=(jax.ShapeDtypeStruct((2, KA * WA,...]
where the time goes in v3:
time: 56.2 us; the launch traced here: 56 us
  Pallas kernels  53.4 us (95%)
  other arithmetic  2.02 us (4%)
  between operations  0.64 us (1%)
    pallas_call x1, Pallas kernels, shards(): pl.pallas_call(main_kernel, out_shape=(jax.ShapeDtypeStruct((2, KA * WA,...  51 us
    pallas_call x1, Pallas kernels, shards(): pl.pallas_call(last_kernel, out_shape=(jax.ShapeDtypeStruct((2, KA * TILE...  2.39 us

profile of v3, /device:TPU:1, one launch (start us, length us, event | category | flops | bytes accessed | tf_op | source)
XLA Modules:
  0.0 56.0 jit_solution(14667499782331598116)
XLA Ops:
  0.6 0.7 %convert_element_type.13 = f32[6]{0:T(128)S(1)} convert(s32[6]{0:T(128)} %param.11) | non-fusion elementwise | flops 6 | bytes 48 | tf_op jit(solution)/shard_map/convert_element_type | solution.py:439
  1.3 0.7 %convert_element_type.12 = f32[256]{0:T(256)S(1)} convert(s32[256]{0:T(256)} %param.12) | non-fusion elementwise | flops 256 | bytes 2048 | tf_op jit(solution)/shard_map/convert_element_type | solution.py:437
  2.0 0.7 %add_bitcast_fusion.small = f32[5,128]{1,0:T(8,128)S(1)} fusion(f32[6]{0:T(128)S(1)} %convert_element_type.13, f32[256]{0:T(256)} %param.13, f32[256]{0:T(256)S(1)} %convert_element_type.12), kind=kLoop, calls=%fused_computation | loop fusion | flops 1280 | bytes 4632 | tf_op jit(solution)/shard_map/reshape | solution.py:440
  2.7 51.0 %mix_and_transform.1 = (bf16[2,128,16,128]{3,2,1,0:T(8,128)(2,1)S(1)}, bf16[48,16,128]{2,1,0:T(8,128)(2,1)S(1)}, bf16[2,32,9600]{2,1,0:T(8,128)(2,1)S(1)}, f32[8,128]{1,0:T(8,128)S(1)}) custom-call(f32[5,128]{1,0:T(8,128)S(1)} %add_bitcast_fusion.small, bf16[6,2,32,9600]{3,2,1,0:T(8,128)(2,1)} %sig_hist.1, bf16[6,2,32,9600]{3,2,1,0:T(8,128)(2,1)} %res_hist.1, ...), custom_call_target="tpu_custom_call" | custom-call | tf_op jit(solution)/shard_map/mix_and_transform/pallas_call | solution.py:441
  53.6 2.4 %unpack.1 = (f32[2,2400,128]{2,1,0:T(8,128)}, bf16[2,32,9600]{2,1,0:T(8,128)(2,1)}, f32[6]{0:T(128)}) custom-call(bf16[2,128,16,128]{3,2,1,0:T(8,128)(2,1)S(1)} %get-tuple-element.10.own, bf16[48,16,128]{2,1,0:T(8,128)(2,1)S(1)} %get-tuple-element.11.own_extra, bf16[2,32,9600]{2,1,0:T(8,128)(2,1)S(1)} %get-tuple-element.12.mixed, ...), custom_call_target="tpu_custom_call" | custom-call | tf_op jit(solution)/shard_map/unpack/pallas_call | solution.py:480

commit v4 on v3

--- a/solution.py
+++ b/solution.py
@@ -18,8 +18,8 @@
 TILES = 75
 UNIT = 512
 WIDTH = TILES * 128
-GRAM_PARTS = ((0, 50), (50, 25))
 GRAM_STEP = 25
+GRAM_STEPS = TILES // GRAM_STEP
 EXTRA = 3
 EXTRA_START = (64, 68, 71)
 
@@ -37,9 +37,9 @@
     return -sine(z.astype(F32) * (math.pi / 512))
 
 
-def build_transform(small, table):
-    odd_freq = 2 * jnp.concatenate([small[0:1], small[1:2]], axis=1).astype(jnp.int32) + 1
-    weight = jnp.concatenate([small[2:3], small[3:4]], axis=1)
+def build_transform(small, weight_ref, table):
+    odd_freq = 2 * jnp.concatenate([small[0:1], small[1:2]], axis=1) + 1
+    weight = weight_ref[...].reshape(1, NTAU)
 
     def block(b, _):
         row = b * 64 + lax.broadcasted_iota(jnp.int32, (64, NTAU), 0)
@@ -106,7 +106,7 @@
 
 
 def main_kernel(
-    small, sig_hist, res_hist, sig_new, res_new,
+    small, weight_ref, sig_hist, res_hist, sig_new, res_new,
     own, own_extra, mixed_out, coef_out,
     sig_v, res_v, sign_v, resn_v, acc, weights, gx, gy, table, regroup,
     mixed, spectra, turned,
@@ -126,15 +126,16 @@
     def arrived(ref, sem):
         pltpu.make_async_copy(ref, ref, sem).wait()
 
-    reads = []
-    for n, (start, size) in enumerate(GRAM_PARTS):
-        cols = pl.ds(start * 128, size * 128)
-        reads.append(
-            (
-                pltpu.make_async_copy(res_hist.at[:, :, :, cols], res_v.at[:, :, :, cols], in_sem.at[0, n]),
-                pltpu.make_async_copy(res_new.at[:, :, cols], resn_v.at[:, :, cols], in_sem.at[1, n]),
-            )
+    def gram_cols(n):
+        return pl.ds(pl.multiple_of(n * (GRAM_STEP * 128), 128), GRAM_STEP * 128)
+
+    def gram_reads(n):
+        cols = gram_cols(n)
+        return (
+            pltpu.make_async_copy(res_hist.at[:, :, :, cols], res_v.at[:, :, :, cols], in_sem.at[0, n]),
+            pltpu.make_async_copy(res_new.at[:, :, cols], resn_v.at[:, :, cols], in_sem.at[1, n]),
         )
+
     sigma_reads = []
     for n, (start, size) in enumerate(((8192, 1408), (0, 4096), (4096, 4096))):
         cols = pl.ds(start, size)
@@ -144,8 +145,8 @@
                 pltpu.make_async_copy(sig_new.at[:, :, cols], sign_v.at[:, :, cols], in_sem.at[3, n]),
             )
         )
-    for group in reads:
-        for read in group:
+    for n in range(GRAM_STEPS):
+        for read in gram_reads(n):
             read.start()
 
     barrier = pltpu.get_barrier_semaphore()
@@ -162,22 +163,21 @@
     lax.fori_loop(1, KA, greet_ka, 0)
 
     acc[...] = jnp.zeros_like(acc)
-    for n, (start, size) in enumerate(GRAM_PARTS):
-        for read in reads[n]:
+
+    def add_products(n):
+        for read in gram_reads(n):
             read.wait()
-
-        def add_products(b, start=start):
-            cols = pl.ds(pl.multiple_of((start + b * GRAM_STEP) * 128, 128), GRAM_STEP * 128)
-            total = None
-            for ri in range(2):
-                block = jnp.concatenate(
-                    [res_v[:, ri, :, cols].reshape(HIST * ROWS, GRAM_STEP * 128), resn_v[ri, :, cols]], axis=0
-                )
-                product = lax.dot_general(block, block, (((1,), (1,)), ((), ())), preferred_element_type=F32)
-                total = product if total is None else total + product
-            acc[...] += total
-
-        each(0, size // GRAM_STEP, add_products)
+        cols = gram_cols(n)
+        total = None
+        for ri in range(2):
+            block = jnp.concatenate(
+                [res_v[:, ri, :, cols].reshape(HIST * ROWS, GRAM_STEP * 128), resn_v[ri, :, cols]], axis=0
+            )
+            product = lax.dot_general(block, block, (((1,), (1,)), ((), ())), preferred_element_type=F32)
+            total = product if total is None else total + product
+        acc[...] += total
+
+    each(0, GRAM_STEPS, add_products)
     for pair in sigma_reads:
         for read in pair:
             read.start()
@@ -207,8 +207,6 @@
             device_id=((k + d) % KA, i), device_id_type=MESH)
 
     each(1, WA, lambda d: share_wa(d).start())
-    build_transform(small, table)
-    build_regroup(regroup)
     for n in range(2):
         arrived(gx.at[: WA - 1], share_sem.at[n])
     total = gx[0]
@@ -216,13 +214,15 @@
         total = total + gx[n]
     gy[k] = total
     each(1, KA, lambda d: share_ka(d).start())
+    build_transform(small, weight_ref, table)
+    build_regroup(regroup)
     for n in range(2, 4):
         arrived(gy.at[: KA - 1], share_sem.at[n])
     gram = gy[0]
     for n in range(1, KA):
         gram = gram + gy[n]
 
-    oldest = jnp.broadcast_to(small[4:5, 0:1], (8, 128))
+    oldest = jnp.broadcast_to(small[2:3, 0:1], (8, 128))
     coeffs = solve(gram, oldest)
     lane = lax.broadcasted_iota(jnp.int32, (8, 128), 1)
     packed = jnp.zeros((8, 128), F32)
@@ -304,15 +304,15 @@
             unit = c * WA + (i + d) % WA
             mix(unit, unit * UNIT)
 
-            @pl.when(d == 0)
+            @pl.when(d == WA)
             def _():
                 unit_keep(c).start()
 
-            @pl.when(d != 0)
+            @pl.when(d != WA)
             def _():
                 unit_copy(c, d).start()
 
-        each(0, WA, send_unit)
+        each(1, WA + 1, send_unit)
     for write in writes:
         write.start()
 
@@ -433,11 +433,7 @@
     vmem = pl.BlockSpec(memory_space=pltpu.VMEM)
     hbm = pl.BlockSpec(memory_space=pltpu.HBM)
     dma = pltpu.SemaphoreType.DMA
-    small = (
-        jnp.pad(freq_index.astype(F32), (0, 384))
-        + jnp.pad(freq_weight, (256, 128))
-        + jnp.pad(slot_order.astype(F32), (512, 128 - HIST))
-    ).reshape(5, 128)
+    small = (jnp.pad(freq_index, (0, 128)) + jnp.pad(slot_order, (NTAU, 128 - HIST))).reshape(3, 128)
     own, own_extra, mixed, coeffs = pl.pallas_call(
         main_kernel,
         out_shape=(
@@ -446,7 +442,7 @@
             jax.ShapeDtypeStruct(sigma_new.shape, BF16),
             jax.ShapeDtypeStruct((8, 128), F32),
         ),
-        in_specs=[vmem] + [hbm] * 4,
+        in_specs=[vmem] * 2 + [hbm] * 4,
         out_specs=(hbm, hbm, hbm, vmem),
         scratch_shapes=[
             pltpu.VMEM(sigma_hist.shape, BF16),
@@ -476,7 +472,7 @@
             collective_id=0, has_side_effects=True, vmem_limit_bytes=51 * 2**20
         ),
         name="mix_and_transform",
-    )(small, sigma_hist, resid_hist, sigma_new, resid_new)
+    )(small, freq_weight, sigma_hist, resid_hist, sigma_new, resid_new)
     out, mixed_sigma, diis_coeffs = pl.pallas_call(
         last_kernel,
         out_shape=(

time: 56.2 us -> 54.5 us (0.970)
  other arithmetic: 2.02 us -> 0.7 us
  Pallas kernels: 53.4 us -> 52.3 us
  local copies, waits for them, and re-layouts: 0 us -> 0.68 us
    convert_element_type x2 -> x0, other arithmetic: 1.34 us -> none  [the longest x1 0.68 us: shards(): freq_index.astype(F32)]
    pallas_call x1, Pallas kernels: 51 us -> 49.9 us  [shards(): pl.pallas_call(main_kernel, out_shape=(jax.ShapeDtypeStruct((2, KA * WA,...]
    unnamed x0 -> x2, local copies, waits for them, and re-layouts: none -> 0.68 us
where the time goes in v4:
time: 54.5 us; the launch traced here: 54.3 us
  Pallas kernels  52.3 us (96%)
  other arithmetic  0.7 us (1%)
  local copies, waits for them, and re-layouts  0.68 us (1%)
  between operations  0.64 us (1%)
    pallas_call x1, Pallas kernels, shards(): pl.pallas_call(main_kernel, out_shape=(jax.ShapeDtypeStruct((2, KA * WA,...  49.9 us
    pallas_call x1, Pallas kernels, shards(): pl.pallas_call(last_kernel, out_shape=(jax.ShapeDtypeStruct((2, KA * TILE...  2.39 us

profile of v4, /device:TPU:1, one launch (start us, length us, event | category | flops | bytes accessed | tf_op | source)
XLA Modules:
  0.0 54.3 jit_solution(239281225394090873)
XLA Ops:
  0.6 0.7 %add_bitcast_fusion.small = s32[3,128]{1,0:T(4,128)S(1)} fusion(s32[6]{0:T(128)} %param.11, s32[256]{0:T(256)} %param.12), kind=kLoop, calls=%fused_computation | loop fusion | flops 384 | bytes 2584 | tf_op jit(solution)/shard_map/reshape | solution.py:436
  1.3 0.0 copy-start
  1.3 0.7 %copy-done = f32[256]{0:T(256)S(1)} copy-done((f32[256]{0:T(256)S(1)}, f32[256]{0:T(256)}, u32[]{:S(2)}) %copy-start) | copy-done | bytes 1048
  2.0 49.9 %mix_and_transform.1 = (bf16[2,128,16,128]{3,2,1,0:T(8,128)(2,1)S(1)}, bf16[48,16,128]{2,1,0:T(8,128)(2,1)S(1)}, bf16[2,32,9600]{2,1,0:T(8,128)(2,1)S(1)}, f32[8,128]{1,0:T(8,128)S(1)}) custom-call(s32[3,128]{1,0:T(4,128)S(1)} %add_bitcast_fusion.small, f32[256]{0:T(256)S(1)} %copy-done, bf16[6,2,32,9600]{3,2,1,0:T(8,128)(2,1)} %sig_hist.1, ...), custom_call_target="tpu_custom_call" | custom-call | tf_op jit(solution)/shard_map/mix_and_transform/pallas_call | solution.py:437
  52.0 2.4 %unpack.1 = (f32[2,2400,128]{2,1,0:T(8,128)}, bf16[2,32,9600]{2,1,0:T(8,128)(2,1)}, f32[6]{0:T(128)}) custom-call(bf16[2,128,16,128]{3,2,1,0:T(8,128)(2,1)S(1)} %get-tuple-element.10.own, bf16[48,16,128]{2,1,0:T(8,128)(2,1)S(1)} %get-tuple-element.11.own_extra, bf16[2,32,9600]{2,1,0:T(8,128)(2,1)S(1)} %get-tuple-element.12.mixed, ...), custom_call_target="tpu_custom_call" | custom-call | tf_op jit(solution)/shard_map/unpack/pallas_call | solution.py:476
Async XLA Ops:
  1.3 0.7 %copy-start = (f32[256]{0:T(256)S(1)}, f32[256]{0:T(256)}, u32[]{:S(2)}) copy-start(f32[256]{0:T(256)} %weight_ref.1) | copy-start | bytes 3076

commit v5 on v4

--- a/solution.py
+++ b/solution.py
@@ -37,9 +37,9 @@
     return -sine(z.astype(F32) * (math.pi / 512))
 
 
-def build_transform(small, weight_ref, table):
-    odd_freq = 2 * jnp.concatenate([small[0:1], small[1:2]], axis=1) + 1
-    weight = weight_ref[...].reshape(1, NTAU)
+def build_transform(small, table):
+    odd_freq = 2 * jnp.concatenate([small[0:1], small[1:2]], axis=1).astype(jnp.int32) + 1
+    weight = jnp.concatenate([small[2:3], small[3:4]], axis=1)
 
     def block(b, _):
         row = b * 64 + lax.broadcasted_iota(jnp.int32, (64, NTAU), 0)
@@ -106,7 +106,7 @@
 
 
 def main_kernel(
-    small, weight_ref, sig_hist, res_hist, sig_new, res_new,
+    small, sig_hist, res_hist, sig_new, res_new,
     own, own_extra, mixed_out, coef_out,
     sig_v, res_v, sign_v, resn_v, acc, weights, gx, gy, table, regroup,
     mixed, spectra, turned,
@@ -214,7 +214,7 @@
         total = total + gx[n]
     gy[k] = total
     each(1, KA, lambda d: share_ka(d).start())
-    build_transform(small, weight_ref, table)
+    build_transform(small, table)
     build_regroup(regroup)
     for n in range(2, 4):
         arrived(gy.at[: KA - 1], share_sem.at[n])
@@ -222,7 +222,7 @@
     for n in range(1, KA):
         gram = gram + gy[n]
 
-    oldest = jnp.broadcast_to(small[2:3, 0:1], (8, 128))
+    oldest = jnp.broadcast_to(small[4:5, 0:1], (8, 128))
     coeffs = solve(gram, oldest)
     lane = lax.broadcasted_iota(jnp.int32, (8, 128), 1)
     packed = jnp.zeros((8, 128), F32)
@@ -316,34 +316,31 @@
     for write in writes:
         write.start()
 
-    def transform(c):
-        def block(b):
-            values = jnp.dot(
-                table[pl.ds(pl.multiple_of(b * 128, 128), 128)],
-                spectra[c].reshape(2 * NTAU, UNIT),
-                preferred_element_type=F32,
-            ).astype(BF16)
-            stacked = jnp.concatenate(
-                [
-                    jnp.concatenate(
-                        [values[n * 32 : (n + 1) * 32, a * 128 : (a + 1) * 128] for a in range(4)], axis=0
-                    )
-                    for n in range(4)
-                ],
-                axis=1,
-            )
-            grouped = jnp.dot(regroup[...], stacked, preferred_element_type=F32).astype(BF16)
-            for n in range(4):
-                turned[c, pl.ds((4 * b + n) * WA, WA)] = grouped[:, n * 128 : (n + 1) * 128].reshape(WA, 16, 128)
-
-        each(0, 4, block)
+    def transform(c, b):
+        values = jnp.dot(
+            table[pl.ds(pl.multiple_of(b * 128, 128), 128)],
+            spectra[c].reshape(2 * NTAU, UNIT),
+            preferred_element_type=F32,
+        ).astype(BF16)
+        stacked = jnp.concatenate(
+            [
+                jnp.concatenate(
+                    [values[n * 32 : (n + 1) * 32, a * 128 : (a + 1) * 128] for a in range(4)], axis=0
+                )
+                for n in range(4)
+            ],
+            axis=1,
+        )
+        grouped = jnp.dot(regroup[...], stacked, preferred_element_type=F32).astype(BF16)
+        for n in range(4):
+            turned[c, pl.ds((4 * b + n) * WA, WA)] = grouped[:, n * 128 : (n + 1) * 128].reshape(WA, 16, 128)
 
     me = k * WA + i
     extra_m = (x - y + 4) % 4
     is_owner = jnp.logical_and(z % 2 == core, extra_m < EXTRA)
 
     def times_copy(c, n):
-        d = KA * WA - n
+        d = KA * WA - 1 - n
         pk = (z + d // 32) % 4 * 4 + (y + d // 8 % 4) % 4
         pi = (x + d // 2 % 4) % 4 * 2 + (core + d % 2) % 2
         target = own_extra.at[k * EXTRA + extra_m] if c == 2 else own.at[c, me]
@@ -356,8 +353,11 @@
         return pltpu.make_async_copy(turned.at[c, me], target, local_sem.at[1, c])
 
     def send_times(c):
-        transform(c)
-        each(1, KA * WA, lambda n: times_copy(c, n).start())
+        def to_z(q):
+            transform(c, (z + 3 - q) % 4)
+            each(32 * q, 32 * (q + 1) - q // 3, lambda n: times_copy(c, n).start())
+
+        each(0, 4, to_z)
         times_keep(c).start()
 
     @pl.when(is_owner)
@@ -433,7 +433,8 @@
     vmem = pl.BlockSpec(memory_space=pltpu.VMEM)
     hbm = pl.BlockSpec(memory_space=pltpu.HBM)
     dma = pltpu.SemaphoreType.DMA
-    small = (jnp.pad(freq_index, (0, 128)) + jnp.pad(slot_order, (NTAU, 128 - HIST))).reshape(3, 128)
+    whole = jnp.pad(freq_index, (0, 384)) + jnp.pad(slot_order, (2 * NTAU, 128 - HIST))
+    small = (whole.astype(F32) + jnp.pad(freq_weight, (NTAU, 128))).reshape(5, 128)
     own, own_extra, mixed, coeffs = pl.pallas_call(
         main_kernel,
         out_shape=(
@@ -442,7 +443,7 @@
             jax.ShapeDtypeStruct(sigma_new.shape, BF16),
             jax.ShapeDtypeStruct((8, 128), F32),
         ),
-        in_specs=[vmem] * 2 + [hbm] * 4,
+        in_specs=[vmem] + [hbm] * 4,
         out_specs=(hbm, hbm, hbm, vmem),
         scratch_shapes=[
             pltpu.VMEM(sigma_hist.shape, BF16),
@@ -472,7 +473,7 @@
             collective_id=0, has_side_effects=True, vmem_limit_bytes=51 * 2**20
         ),
         name="mix_and_transform",
-    )(small, freq_weight, sigma_hist, resid_hist, sigma_new, resid_new)
+    )(small, sigma_hist, resid_hist, sigma_new, resid_new)
     out, mixed_sigma, diis_coeffs = pl.pallas_call(
         last_kernel,
         out_shape=(

time: 54.5 us -> 53.7 us (0.985)
  local copies, waits for them, and re-layouts: 0.68 us -> 0 us
    unnamed x2 -> x0, local copies, waits for them, and re-layouts: 0.68 us -> none
where the time goes in v5:
time: 53.7 us; the launch traced here: 53.6 us
  Pallas kernels  52.2 us (97%)
  other arithmetic  0.72 us (1%)
  between operations  0.64 us (1%)
    pallas_call x1, Pallas kernels, shards(): pl.pallas_call(main_kernel, out_shape=(jax.ShapeDtypeStruct((2, KA * WA,...  49.8 us
    pallas_call x1, Pallas kernels, shards(): pl.pallas_call(last_kernel, out_shape=(jax.ShapeDtypeStruct((2, KA * TILE...  2.39 us

profile of v5, /device:TPU:1, one launch (start us, length us, event | category | flops | bytes accessed | tf_op | source)
XLA Modules:
  0.0 53.6 jit_solution(5256226391049404751)
XLA Ops:
  0.6 0.7 %add_bitcast_fusion.small = f32[5,128]{1,0:T(8,128)S(1)} fusion(f32[256]{0:T(256)} %param.13, s32[6]{0:T(128)} %param.11, s32[256]{0:T(256)} %param.12), kind=kLoop, calls=%fused_computation | loop fusion | flops 1920 | bytes 4632 | tf_op jit(solution)/shard_map/reshape | solution.py:437
  1.4 49.8 %mix_and_transform.1 = (bf16[2,128,16,128]{3,2,1,0:T(8,128)(2,1)S(1)}, bf16[48,16,128]{2,1,0:T(8,128)(2,1)S(1)}, bf16[2,32,9600]{2,1,0:T(8,128)(2,1)S(1)}, f32[8,128]{1,0:T(8,128)S(1)}) custom-call(f32[5,128]{1,0:T(8,128)S(1)} %add_bitcast_fusion.small, bf16[6,2,32,9600]{3,2,1,0:T(8,128)(2,1)} %sig_hist.1, bf16[6,2,32,9600]{3,2,1,0:T(8,128)(2,1)} %res_hist.1, ...), custom_call_target="tpu_custom_call" | custom-call | tf_op jit(solution)/shard_map/mix_and_transform/pallas_call | solution.py:438
  51.2 2.4 %unpack.1 = (f32[2,2400,128]{2,1,0:T(8,128)}, bf16[2,32,9600]{2,1,0:T(8,128)(2,1)}, f32[6]{0:T(128)}) custom-call(bf16[2,128,16,128]{3,2,1,0:T(8,128)(2,1)S(1)} %get-tuple-element.10.own, bf16[48,16,128]{2,1,0:T(8,128)(2,1)S(1)} %get-tuple-element.11.own_extra, bf16[2,32,9600]{2,1,0:T(8,128)(2,1)S(1)} %get-tuple-element.12.mixed, ...), custom_call_target="tpu_custom_call" | custom-call | tf_op jit(solution)/shard_map/unpack/pallas_call | solution.py:477

commit v6 on v5

--- a/solution.py
+++ b/solution.py
@@ -65,7 +65,7 @@
 
 def solve(gram, oldest):
     def entry(s, u):
-        return jnp.broadcast_to(gram[s : s + 1, u : u + 1], (8, 128))
+        return jnp.broadcast_to(gram[:, 16 * s + u : 16 * s + u + 1], (8, 128))
 
     full = {(s, u): entry(s, u) for s in range(HIST + 1) for u in range(s + 1)}
     mat = {}
@@ -187,12 +187,14 @@
     by_lane = jnp.sum(kept.reshape(7, ROWS, 7 * ROWS), axis=1)
     fold = jnp.where(
         lax.broadcasted_iota(jnp.int32, (7 * ROWS, 128), 0) // ROWS
-        == lax.broadcasted_iota(jnp.int32, (7 * ROWS, 128), 1),
+        == lax.broadcasted_iota(jnp.int32, (7 * ROWS, 128), 1) % 16,
         1.0,
         0.0,
     )
     share = jnp.dot(by_lane, fold, preferred_element_type=F32, precision=lax.Precision.HIGHEST)
-    gx[i] = jnp.concatenate([share, jnp.zeros((1, 128), F32)], axis=0)
+    row = lax.broadcasted_iota(jnp.int32, (7, 128), 0)
+    group = lax.broadcasted_iota(jnp.int32, (7, 128), 1) // 16
+    gx[i] = jnp.sum(jnp.where(row == group, share, 0.0), axis=0, keepdims=True)
 
     pl.semaphore_wait(barrier, WA - 1 + KA - 1)
 
@@ -452,8 +454,8 @@
             pltpu.VMEM(resid_new.shape, BF16),
             pltpu.VMEM((7 * ROWS, 7 * ROWS), F32),
             pltpu.VMEM((HIST + 1, 8, 128), F32),
-            pltpu.VMEM((WA, 8, 128), F32),
-            pltpu.VMEM((KA, 8, 128), F32),
+            pltpu.VMEM((WA, 1, 128), F32),
+            pltpu.VMEM((KA, 1, 128), F32),
             pltpu.VMEM((2 * NTAU, 2 * NTAU), BF16),
             pltpu.VMEM((128, 128), BF16),
             pltpu.VMEM((2 * WA + EXTRA, 2, ROWS, UNIT), BF16),

time: 53.7 us -> 53.1 us (0.989)
  Pallas kernels: 52.2 us -> 51.6 us
    pallas_call x1, Pallas kernels: 49.8 us -> 49.2 us  [shards(): pl.pallas_call(main_kernel, out_shape=(jax.ShapeDtypeStruct((2, KA * WA,...]
where the time goes in v6:
time: 53.1 us; the launch traced here: 53 us
  Pallas kernels  51.6 us (97%)
  other arithmetic  0.72 us (1%)
  between operations  0.64 us (1%)
    pallas_call x1, Pallas kernels, shards(): pl.pallas_call(main_kernel, out_shape=(jax.ShapeDtypeStruct((2, KA * WA,...  49.2 us
    pallas_call x1, Pallas kernels, shards(): pl.pallas_call(last_kernel, out_shape=(jax.ShapeDtypeStruct((2, KA * TILE...  2.39 us

profile of v6, /device:TPU:1, one launch (start us, length us, event | category | flops | bytes accessed | tf_op | source)
XLA Modules:
  0.0 53.0 jit_solution(7098943566830713357)
XLA Ops:
  0.6 0.7 %add_bitcast_fusion.small = f32[5,128]{1,0:T(8,128)S(1)} fusion(f32[256]{0:T(256)} %param.13, s32[6]{0:T(128)} %param.11, s32[256]{0:T(256)} %param.12), kind=kLoop, calls=%fused_computation | loop fusion | flops 1920 | bytes 4632 | tf_op jit(solution)/shard_map/reshape | solution.py:439
  1.4 49.2 %mix_and_transform.1 = (bf16[2,128,16,128]{3,2,1,0:T(8,128)(2,1)S(1)}, bf16[48,16,128]{2,1,0:T(8,128)(2,1)S(1)}, bf16[2,32,9600]{2,1,0:T(8,128)(2,1)S(1)}, f32[8,128]{1,0:T(8,128)S(1)}) custom-call(f32[5,128]{1,0:T(8,128)S(1)} %add_bitcast_fusion.small, bf16[6,2,32,9600]{3,2,1,0:T(8,128)(2,1)} %sig_hist.1, bf16[6,2,32,9600]{3,2,1,0:T(8,128)(2,1)} %res_hist.1, ...), custom_call_target="tpu_custom_call" | custom-call | tf_op jit(solution)/shard_map/mix_and_transform/pallas_call | solution.py:440
  50.6 2.4 %unpack.1 = (f32[2,2400,128]{2,1,0:T(8,128)}, bf16[2,32,9600]{2,1,0:T(8,128)(2,1)}, f32[6]{0:T(128)}) custom-call(bf16[2,128,16,128]{3,2,1,0:T(8,128)(2,1)S(1)} %get-tuple-element.10.own, bf16[48,16,128]{2,1,0:T(8,128)(2,1)S(1)} %get-tuple-element.11.own_extra, bf16[2,32,9600]{2,1,0:T(8,128)(2,1)S(1)} %get-tuple-element.12.mixed, ...), custom_call_target="tpu_custom_call" | custom-call | tf_op jit(solution)/shard_map/unpack/pallas_call | solution.py:479
